TPU v7x, 32 devices: a whole 2x2x4 slice. The times are simulated.
32 devices in a mesh: wide: 8 (over z, x), narrow: 4 (over y, core).
Axes of the slice: x: 2, y: 2, z: 4, core: 2. Of those that a mesh axis runs over, the one named last changes fastest.
Arguments:
- jacobian: bfloat16 [2048, 16384], P(None, ('wide', 'narrow')), may hold values from -0.125 to 0.125
- variance: float32 [2048], replicated, may hold values from 0.1 to 10
Outputs:
- hessian: float32 [16384, 16384], P('wide', 'narrow')
All inputs are finite; a program needn't handle non-finite values.
Results may differ from a plain program's by a relative error of at most 0.004.
Values may be sent and summed in bfloat16 or wider, within the bound.
No kernel may reach another device: no remote copies, remote signals or barrier semaphores. Data moves between devices by JAX's collectives and lax.ppermute only.
A program may use at most 128 MiB of HBM per device.

v0:
```python
import jax
import jax.numpy as jnp
from jax import lax
from jax.experimental import pallas as pl
from jax.experimental.pallas import tpu as pltpu
from jax.sharding import PartitionSpec as P

AXES = ("wide", "narrow")
CORES = 2
LANES = 128
PARTS = 2
TURN = 512
VMEM_MIB = 24


class Layout:
    def __init__(self, mesh):
        self.wide, self.narrow = mesh.shape["wide"], mesh.shape["narrow"]
        self.xs = self.wide // self.narrow
        self.zs = self.narrow
        self.ys = self.narrow // CORES
        self.sites = [
            (z, x, y, c)
            for z in range(self.zs)
            for x in range(self.xs)
            for y in range(self.ys)
            for c in range(CORES)
        ]

    def index(self, z, x, y, c):
        return ((z * self.xs + x) * self.ys + y) * CORES + c

    def moves(self, target):
        pairs = []
        for site in self.sites:
            to = target(*site)
            if to is not None:
                pairs.append((self.index(*site), self.index(*to)))
        return pairs


def weigh(panel, row_scale):
    return (panel.astype(jnp.float32) * row_scale).astype(jnp.bfloat16)


def inner(z):
    return (z % 4 == 1) | (z % 4 == 2)


def apart(z, y):
    return (z // CORES) ^ y


def choose(options, index):
    picked = options[0]
    for at in range(1, len(options)):
        picked = jnp.where(index == at, options[at], picked)
    return picked


def to_mate(z, x, y, c):
    return z, x, y, 1 - c


def to_pair(z, x, y, c):
    return z ^ 1, x, y, c


def to_cross(z, x, y, c):
    return (z ^ 3, x, y, c) if inner(z) else None


def to_outer(z, x, y, c):
    return (z ^ 1, x, y, c) if inner(z) else None


def to_back(z, x, y, c):
    return (z, x, y ^ 1, c) if apart(z, y) == 0 else None


def to_far(q):
    return lambda z, x, y, c: (z ^ (CORES * q), x, y, c)


def along_y(m):
    return lambda z, x, y, c: (z, x, y ^ m, c)


def along_x(lay, s, who=lambda z, y: True):
    return lambda z, x, y, c: (z, (x + s) % lay.xs, y, c) if who(z, y) else None


def turn(rows, chunks, at, shape):
    depth, step = chunks[0].shape

    def kernel(*refs):
        chunk_refs, out_ref, token_ref = refs[: len(chunks)], refs[-2], refs[-1]
        for k, ref in enumerate(chunk_refs):
            out_ref[k * step : (k + 1) * step, :] = ref[...].T
        token_ref[...] = jnp.zeros_like(token_ref)

    operands = list(chunks)
    in_specs = [pl.BlockSpec((TURN, step), lambda i: (i, 0)) for _ in chunks]
    aliases = {}
    if rows is not None:
        operands.append(rows)
        in_specs.append(pl.BlockSpec(memory_space=pl.ANY))
        aliases = {len(operands) - 1: 0}
    return pl.pallas_call(
        kernel,
        grid=(depth // TURN,),
        in_specs=in_specs,
        out_specs=[
            pl.BlockSpec((step * len(chunks), TURN), lambda i: (at, i)),
            pl.BlockSpec((8, LANES), lambda i: (0, 0)),
        ],
        out_shape=[
            jax.ShapeDtypeStruct(shape, jnp.bfloat16),
            jax.ShapeDtypeStruct((8, LANES), jnp.float32),
        ],
        input_output_aliases=aliases,
        compiler_params=pltpu.CompilerParams(vmem_limit_bytes=VMEM_MIB * 2**20),
        cost_estimate=pl.CostEstimate(
            flops=0, bytes_accessed=4 * depth * step * len(chunks), transcendentals=0
        ),
    )(*operands)


def multiply(tile, rows, chunks, blocks, place, shape, band):
    high, depth = rows.shape
    step, count = chunks[0].shape[1], len(chunks)
    bands = high // band

    def kernel(blocks_ref, place_ref, rows_ref, *refs):
        chunk_refs = refs[:count]
        tile_ref, token_ref, result, sems = refs[-4:]
        i = pl.program_id(0)

        def copies(i):
            at = pl.multiple_of((i ^ place_ref[0]) * band, band)
            return [
                pltpu.make_async_copy(
                    result.at[i % 2, :, k * step : (k + 1) * step],
                    tile_ref.at[pl.ds(at, band), pl.ds(pl.multiple_of(blocks_ref[k] * step, step), step)],
                    sems.at[i % 2, k],
                )
                for k in range(count)
            ]

        @pl.when(i >= 2)
        def _():
            for copy in copies(i - 2):
                copy.wait()

        right = jnp.concatenate([ref[...] for ref in chunk_refs], axis=1)
        result[i % 2] = jnp.dot(rows_ref[...], right, preferred_element_type=jnp.float32)
        for copy in copies(i):
            copy.start()

        @pl.when(i == bands - 1)
        def _():
            token_ref[...] = jnp.zeros_like(token_ref)
            for last in range(max(bands - 2, 0), bands):
                for copy in copies(last):
                    copy.wait()

    operands = [rows, *chunks]
    in_specs = [pl.BlockSpec((band, depth), lambda i, b, p: (i, 0))]
    in_specs += [pl.BlockSpec((depth, step), lambda i, b, p: (0, 0)) for _ in chunks]
    aliases = {}
    if tile is not None:
        operands.append(tile)
        in_specs.append(pl.BlockSpec(memory_space=pl.ANY))
        aliases = {len(operands) + 1: 0}
    return pl.pallas_call(
        kernel,
        grid_spec=pltpu.PrefetchScalarGridSpec(
            num_scalar_prefetch=2,
            grid=(bands,),
            in_specs=in_specs,
            out_specs=[
                pl.BlockSpec(memory_space=pl.ANY),
                pl.BlockSpec((8, LANES), lambda i, b, p: (0, 0)),
            ],
            scratch_shapes=[
                pltpu.VMEM((2, band, step * count), jnp.float32),
                pltpu.SemaphoreType.DMA((2, count)),
            ],
        ),
        out_shape=[
            jax.ShapeDtypeStruct(shape, jnp.float32),
            jax.ShapeDtypeStruct((8, LANES), jnp.float32),
        ],
        input_output_aliases=aliases,
        compiler_params=pltpu.CompilerParams(vmem_limit_bytes=VMEM_MIB * 2**20),
        cost_estimate=pl.CostEstimate(
            flops=2 * high * depth * step * count,
            bytes_accessed=2 * high * depth + (2 * depth + 4 * high) * step * count,
            transcendentals=0,
        ),
    )(jnp.stack(blocks), place[None], *operands)


def solution(mesh):
    lay = Layout(mesh)

    def body(jacobian, variance):
        depth, width = jacobian.shape
        step = width // PARTS
        shape = (lay.narrow * width, lay.xs * lay.narrow * width)
        wide_at, narrow_at = lax.axis_index("wide"), lax.axis_index("narrow")
        z, x = wide_at // lay.xs, wide_at % lay.xs
        y, c = narrow_at // CORES, narrow_at % CORES
        is_inner, off = inner(z), apart(z, y)
        home, beside = off == 0, off == 1
        halves, others, shifts = range(2, lay.zs // CORES), range(1, lay.ys), range(1, lay.xs)
        first_kept = ((z % CORES) ^ (is_inner & beside)) == c

        row_scale = lax.rsqrt(variance)[:, None]
        got = {}
        for h in range(PARTS):
            got["own", h] = weigh(jacobian[:, h * step : (h + 1) * step], row_scale)
        running = []

        def across(kind, h):
            return jnp.where(is_inner, got[kind + "_cross", h], got[kind + "_outer", h])

        def first(h, q):
            options = [got["own", h], across("own", h)] + [got["far_own", h, n] for n in halves]
            return choose(options, q)

        def second(h, q):
            options = [got["pair", h], across("pair", h)] + [got["far_pair", h, n] for n in halves]
            return choose(options, q)

        def send(name, value, target):
            running.append((name, lax.ppermute(value, AXES, lay.moves(target))))

        def settle(barrier=True):
            got.update(running)
            running.clear()
            if barrier:
                got.update(zip(got, lax.optimization_barrier(tuple(got.values()))))


        def pair(h):
            send(("pair", h), got["own", h], to_pair)

        def cross(kind, h):
            send((kind + "_cross", h), got[kind, h], to_cross)
            for n in halves:
                send(("far_" + kind, h, n), got[kind, h], to_far(n))

        def outer(kind, h):
            send((kind + "_outer", h), got[kind + "_cross", h], to_outer)


        def row(h):
            for m in others:
                send(("row", h, m), got["own", h], along_y(m))

        def give(h):
            for m in others:
                value = jnp.where(off == m, got["pair", h], first(h, off ^ m))
                send(("give", h, m), value, along_y(m))

        def give_more(h):
            for m in others:
                value = jnp.where(off == m, got["own_x", h, 1], second(h, off ^ m))
                send(("give_more", h, m), value, along_y(m))

        def own_x(h):
            for s in shifts:
                send(("own_x", h, s), got["own", h], along_x(lay, s))

        def near_x(h):
            value = jnp.where(home, got["pair", h], first(h, off))
            for s in shifts:
                send(("near_x", h, s), value, along_x(lay, s))

        def more_x(h):
            for m in others:
                value = jnp.where(home, got["give", h, m], second(h, off))
                for s in shifts:
                    who = lambda z, y, m=m: m == 1 or apart(z, y) == 0
                    send(("more_x", h, s, m), value, along_x(lay, s, who))
                    rest = lambda z, y, m=m: apart(z, y) > 1 or (apart(z, y) == 1 and m != 1)
                    if lay.ys > 2:
                        send(("rest_x", h, s, m), got["give_more", h, m], along_x(lay, s, rest))

        def give_x(h):
            for m in others:
                value = jnp.where(home, second(h, 1), got["give", h, m])
                for s in shifts:
                    who = lambda z, y, m=m: m == 1 or apart(z, y) != 0
                    send(("give_x", h, s, m), value, along_x(lay, s, who))

        def back(h):
            for s in shifts:
                send(("back", h, s), got["give_x", h, s, 1], to_back)


        def mate(kind, h):
            for name in [n for n in got if n[0] == kind and n[1] == h]:
                send((kind + "_mate", *name[1:]), got[name], to_mate)

        def places(kind):
            return [(s, m) for s in (shifts if "x" in kind else (0,)) for m in (others if "y" in kind else (0,))]

        def both(h, s, m):
            if s == 0 and m == 0:
                return first(h, off), second(h, off)
            if s == 0:
                return (
                    jnp.where(home, got["row", h, m], got["give", h, m]),
                    jnp.where(home, got["give", h, m], got["give_more", h, m]),
                )
            if m == 0:
                return (
                    jnp.where(home, got["own_x", h, s], got["near_x", h, s]),
                    jnp.where(home, got["near_x", h, s], got["more_x", h, s, 1]),
                )
            last = got.get(("rest_x", h, s, m), got["back", h, s])
            if m == 1 and lay.ys > 2:
                last = jnp.where(beside, got["back", h, s], last)
            return (
                jnp.where(home, got["give_more", h, m], got["give_x", h, s, m]),
                jnp.where(home, got["more_x", h, s, m], last),
            )

        def swap(kind, h):
            for s, m in places(kind):
                one, two = both(h, s, m)
                got["kept", h, s, m] = jnp.where(first_kept, one, two)
                send(("swapped", h, s, m), jnp.where(first_kept, two, one), to_mate)


        def lay_row(m, side):
            kind = ("row" if m else "own") + ("_mate" if side else "")
            chunks = [got[(kind, h, m) if m else (kind, h)] for h in range(PARTS)]
            band = m * CORES + side
            if step % LANES:
                rows = got.get("rows")
                rows = jnp.zeros((depth, shape[0]), jnp.bfloat16) if rows is None else rows
                value = jnp.concatenate(chunks, axis=1)
                got["rows"] = lax.dynamic_update_slice(rows, value, (0, (narrow_at ^ band) * width))
            else:
                got["rows"], got["mark", "row", band] = turn(got.get("rows"), chunks, band, (shape[0], depth))

        def product(h, *kinds, sides=(0, 1)):
            chunks, blocks = [], []
            for kind in kinds:
                for s, m in places(kind):
                    for side in sides:
                        chunks.append(got["swapped" if side else "kept", h, s, m])
                        block = ((x - s) % lay.xs * lay.ys + (y ^ m)) * CORES + (c ^ side)
                        blocks.append(block * PARTS + h)
            tile = got.get("tile")
            if step % LANES:
                tile = jnp.zeros(shape, jnp.float32) if tile is None else tile
                for chunk, block in zip(chunks, blocks):
                    dims = (((0,), (0,)), ((), ()))
                    part = lax.dot_general(got["rows"], chunk, dims, preferred_element_type=jnp.float32)
                    tile = lax.dynamic_update_slice(tile, part, (0, block * step))
                got["tile"] = tile
            else:
                got["tile"], got["mark", "tile"] = multiply(tile, got["rows"], chunks, blocks, narrow_at, shape, width)

        pair(0)
        cross("own", 0)
        own_x(0)
        row(0)
        mate("own", 0)
        settle()

        outer("own", 0)
        cross("pair", 0)
        own_x(1)
        row(1)
        mate("own", 1)
        settle()

        outer("pair", 0)
        cross("own", 1)
        near_x(0)
        give(0)
        mate("row", 0)
        lay_row(0, 0)
        settle()

        pair(1)
        give_x(0)
        give_more(0)
        mate("row", 1)
        swap("", 0)
        lay_row(0, 1)
        settle()

        outer("own", 1)
        cross("pair", 1)
        more_x(0)
        back(0)
        swap("y", 0)
        for m in others:
            lay_row(m, 0)
            lay_row(m, 1)
        settle()

        outer("pair", 1)
        near_x(1)
        give(1)
        swap("x", 0)
        swap("xy", 0)
        product(0, "", "y")
        settle()

        give_x(1)
        give_more(1)
        swap("", 1)
        product(0, "x", "xy")
        settle()

        more_x(1)
        back(1)
        swap("y", 1)
        product(1, "")
        settle()

        swap("x", 1)
        swap("xy", 1)
        product(1, "y")
        product(1, "x", "xy", sides=(0,))
        settle()

        product(1, "x", "xy", sides=(1,))
        return got["tile"]

    placed = (P(None, AXES), P())
    return jax.shard_map(
        body, mesh=mesh, in_specs=placed, out_specs=P("wide", "narrow"), check_vma=False
    )
```

profile of v0, /device:TPU:17, one launch (start us, length us, event | category | flops | bytes accessed | tf_op | source)
XLA Modules:
  0.0 278.3 jit_solution(2701493983355861867)
XLA Ops:
  10.0 16.9 %collective-permute-done = bf16[2048,256]{1,0:T(8,128)(2,1)} collective-permute-done((bf16[2048,256]{1,0:T(8,128)(2,1)S(1)}, bf16[2048,256]{1,0:T(8,128)(2,1)}, u32[]{:S(2)}, u32[]{:S(2)}) %collective-permute-start) | collective-permute-done | bytes 1048608 | tf_op jit(solution)/shard_map/ppermute | solution.py:237
  42.2 11.9 %collective-permute-done.5 = bf16[2048,256]{1,0:T(8,128)(2,1)} collective-permute-done((bf16[2048,256]{1,0:T(8,128)(2,1)}, bf16[2048,256]{1,0:T(8,128)(2,1)}, u32[]{:S(2)}, u32[]{:S(2)}) %collective-permute-start.5) | collective-permute-done | bytes 1048608 | tf_op jit(solution)/shard_map/ppermute | solution.py:237
  54.1 4.8 %collective-permute-done.6 = bf16[2048,256]{1,0:T(8,128)(2,1)} collective-permute-done((bf16[2048,256]{1,0:T(8,128)(2,1)}, bf16[2048,256]{1,0:T(8,128)(2,1)}, u32[]{:S(2)}, u32[]{:S(2)}) %collective-permute-start.6) | collective-permute-done | bytes 1048608 | tf_op jit(solution)/shard_map/ppermute | solution.py:237
  69.7 4.7 %collective-permute-start.14 = (bf16[2048,256]{1,0:T(8,128)(2,1)}, bf16[2048,256]{1,0:T(8,128)(2,1)}, u32[]{:S(2)}, u32[]{:S(2)}) collective-permute-start(bf16[2048,256]{1,0:T(8,128)(2,1)} %copy-done.5), channel_id=1, source_target_pairs={{0,1},{1,0},{2,3},{3,2},{4,5},{5,4},{6,7},{7,6},{8,9},{9,8},{10,11... | collective-permute-start | bytes 3145736 | tf_op jit(solution)/shard_map/ppermute | solution.py:237
  75.9 3.9 %collective-permute-done.10 = bf16[2048,256]{1,0:T(8,128)(2,1)} collective-permute-done((bf16[2048,256]{1,0:T(8,128)(2,1)}, bf16[2048,256]{1,0:T(8,128)(2,1)}, u32[]{:S(2)}, u32[]{:S(2)}) %collective-permute-start.10) | collective-permute-done | bytes 1048608 | tf_op jit(solution)/shard_map/ppermute | solution.py:237
  79.7 4.6 %collective-permute-done.11 = bf16[2048,256]{1,0:T(8,128)(2,1)} collective-permute-done((bf16[2048,256]{1,0:T(8,128)(2,1)S(1)}, bf16[2048,256]{1,0:T(8,128)(2,1)}, u32[]{:S(2)}, u32[]{:S(2)}) %collective-permute-start.11) | collective-permute-done | bytes 1048608 | tf_op jit(solution)/shard_map/ppermute | solution.py:237
  84.3 3.8 %collective-permute-done.12 = bf16[2048,256]{1,0:T(8,128)(2,1)} collective-permute-done((bf16[2048,256]{1,0:T(8,128)(2,1)}, bf16[2048,256]{1,0:T(8,128)(2,1)}, u32[]{:S(2)}, u32[]{:S(2)}) %collective-permute-start.12) | collective-permute-done | bytes 1048608 | tf_op jit(solution)/shard_map/ppermute | solution.py:237
  95.6 5.8 %collective-permute-start.18 = (bf16[2048,256]{1,0:T(8,128)(2,1)S(1)}, bf16[2048,256]{1,0:T(8,128)(2,1)S(1)}, u32[]{:S(2)}, u32[]{:S(2)}) collective-permute-start(bf16[2048,256]{1,0:T(8,128)(2,1)S(1)} %collective-permute-done.8.refs_1_), channel_id=1, source_target_pairs={{0,1},{1,0},{2,3},{3,2},{4,5},{5,4},{6,7},{7,6},{8,9},{9,8},{10,11... | collective-permute-start | bytes 3145736 | tf_op jit(solution)/shard_map/ppermute | solution.py:237
  104.6 3.8 %collective-permute-done.15 = bf16[2048,256]{1,0:T(8,128)(2,1)S(1)} collective-permute-done((bf16[2048,256]{1,0:T(8,128)(2,1)S(1)}, bf16[2048,256]{1,0:T(8,128)(2,1)S(1)}, u32[]{:S(2)}, u32[]{:S(2)}) %collective-permute-start.15) | collective-permute-done | bytes 1048608 | tf_op jit(solution)/shard_map/ppermute | solution.py:237
  108.4 4.9 %collective-permute-done.16 = bf16[2048,256]{1,0:T(8,128)(2,1)S(1)} collective-permute-done((bf16[2048,256]{1,0:T(8,128)(2,1)S(1)}, bf16[2048,256]{1,0:T(8,128)(2,1)S(1)}, u32[]{:S(2)}, u32[]{:S(2)}) %collective-permute-start.16) | collective-permute-done | bytes 1048608 | tf_op jit(solution)/shard_map/ppermute | solution.py:237
  125.5 7.7 %collective-permute-start.24 = (bf16[2048,256]{1,0:T(8,128)(2,1)S(1)}, bf16[2048,256]{1,0:T(8,128)(2,1)S(1)}, u32[]{:S(2)}, u32[]{:S(2)}) collective-permute-start(bf16[2048,256]{1,0:T(8,128)(2,1)S(1)} %get-tuple-element.279), channel_id=1, source_target_pairs={{0,1},{1,0},{2,3},{3,2},{4,5},{5,4},{6,7},{7,6},{8,9},{9,8},{10,11... | collective-permute-start | bytes 3145736 | tf_op jit(solution)/shard_map/ppermute | solution.py:237
  148.8 3.6 %broadcast_select_fusion.8 = (bf16[2048,256]{1,0:T(8,128)(2,1)}, bf16[2048,256]{1,0:T(8,128)(2,1)S(1)}, bf16[2048,256]{1,0:T(8,128)(2,1)}, bf16[2048,256]{1,0:T(8,128)(2,1)}) fusion(pred[]{:T(512)S(6)} %eq.60, bf16[2048,256]{1,0:T(8,128)(2,1)S(1)} %collective-permute-done.17, bf16[2048,256]{1,0:T(8,128)(2,1)S(1)} %collective-permute-done.16, pred[]{:T(512)S(6)} %eq.55, ...), kind=kLoop, calls=%fused_computation.20 | loop fusion | flops 4194304 | bytes 10485762 | tf_op jit(solution)/shard_map/jit(_where)/select_n | solution.py:335
  152.5 8.9 %collective-permute-start.28 = (bf16[2048,256]{1,0:T(8,128)(2,1)}, bf16[2048,256]{1,0:T(8,128)(2,1)}, u32[]{:S(2)}, u32[]{:S(2)}) collective-permute-start(bf16[2048,256]{1,0:T(8,128)(2,1)} %get-tuple-element.292), channel_id=1, source_target_pairs={{0,1},{1,0},{2,3},{3,2},{4,5},{5,4},{6,7},{7,6},{8,9},{9,8},{10,11... | collective-permute-start | bytes 3145736 | tf_op jit(solution)/shard_map/ppermute | solution.py:237
  161.5 3.4 %copy-done.1 = bf16[2048,2048]{1,0:T(8,128)(2,1)S(1)} copy-done((bf16[2048,2048]{1,0:T(8,128)(2,1)S(1)}, bf16[2048,2048]{1,0:T(8,128)(2,1)}, u32[]{:S(2)}) %copy-start.1) | copy-done | bytes 8388632
  169.8 11.9 %shard_map.32 = (f32[2048,4096]{1,0:T(8,128)}, f32[8,128]{1,0:T(8,128)}) custom-call(s32[4]{0:T(128)S(1)} %pad_add_fusion.1.blocks_ref, s32[1]{0:T(128)} %bitcast.2.place_ref, bf16[2048,2048]{1,0:T(8,128)(2,1)S(1)} %copy-done.1, bf16[2048,256]{1,0:T(8,128)(2,1)S(1)} %copy-done.10, bf16[2048,256]{1,0:T(8,128)(2,1)S(1)} %copy-done.15, ...), custom_call_target="tpu_custom_call" | custom-call | flops 8589934592 | bytes 20971520 | tf_op jit(solution)/shard_map/pallas_call | solution.py:175
  195.2 13.5 %shard_map.33 = (f32[2048,4096]{1,0:T(8,128)}, f32[8,128]{1,0:T(8,128)}) custom-call(s32[4]{0:T(128)S(1)} %pad_add_fusion.2.blocks_ref, s32[1]{0:T(128)} %bitcast.2.place_ref, bf16[2048,2048]{1,0:T(8,128)(2,1)S(1)} %copy-done.2, bf16[2048,256]{1,0:T(8,128)(2,1)S(1)} %copy-done.7, ...), custom_call_target="tpu_custom_call", output_to_operand_aliasing={{0}: (7, {})} | custom-call | flops 8589934592 | bytes 20971520 | tf_op jit(solution)/shard_map/pallas_call | solution.py:175
  208.7 4.0 %collective-permute-done.30 = bf16[2048,256]{1,0:T(8,128)(2,1)} collective-permute-done((bf16[2048,256]{1,0:T(8,128)(2,1)}, bf16[2048,256]{1,0:T(8,128)(2,1)}, u32[]{:S(2)}, u32[]{:S(2)}) %collective-permute-start.30) | collective-permute-done | bytes 1048608 | tf_op jit(solution)/shard_map/ppermute | solution.py:237
  213.6 3.5 %broadcast_select_fusion.4 = (bf16[2048,256]{1,0:T(8,128)(2,1)}, bf16[2048,256]{1,0:T(8,128)(2,1)S(1)}, bf16[2048,256]{1,0:T(8,128)(2,1)}) fusion(pred[]{:T(512)S(6)} %eq.60, bf16[2048,256]{1,0:T(8,128)(2,1)S(1)} %collective-permute-done.8.refs_1_, bf16[2048,256]{1,0:T(8,128)(2,1)} %collective-permute-done.27, pred[]{:T(512)S(6)} %eq.55, ...), kind=kLoop, calls=%fused_computation.16 | loop fusion | flops 3670016 | bytes 9437188 | tf_op jit(solution)/shard_map/jit(_where)/select_n | solution.py:335
  224.1 8.4 %shard_map.34 = (f32[2048,4096]{1,0:T(8,128)}, f32[8,128]{1,0:T(8,128)}) custom-call(s32[2]{0:T(128)S(1)} %pad_add_fusion.3.blocks_ref, s32[1]{0:T(128)} %bitcast.2.place_ref, bf16[2048,2048]{1,0:T(8,128)(2,1)S(1)} %copy-done.3, bf16[2048,256]{1,0:T(8,128)(2,1)S(1)} %get-tuple-element.233.refs_0_, ...), custom_call_target="tpu_custom_call", output_to_operand_aliasing={{0}: (5, {})} | custom-call | flops 4294967296 | bytes 14680064 | tf_op jit(solution)/shard_map/pallas_call | solution.py:175
  232.5 7.9 %collective-permute-done.33 = bf16[2048,256]{1,0:T(8,128)(2,1)} collective-permute-done((bf16[2048,256]{1,0:T(8,128)(2,1)}, bf16[2048,256]{1,0:T(8,128)(2,1)}, u32[]{:S(2)}, u32[]{:S(2)}) %collective-permute-start.33) | collective-permute-done | bytes 1048608 | tf_op jit(solution)/shard_map/ppermute | solution.py:237
  243.6 4.0 %broadcast_select_fusion = (bf16[2048,256]{1,0:T(8,128)(2,1)}, bf16[2048,256]{1,0:T(8,128)(2,1)S(1)}, bf16[2048,256]{1,0:T(8,128)(2,1)S(1)}, bf16[2048,256]{1,0:T(8,128)(2,1)}) fusion(pred[]{:T(512)S(6)} %eq.60, bf16[2048,256]{1,0:T(8,128)(2,1)} %collective-permute-done.31, bf16[2048,256]{1,0:T(8,128)(2,1)} %collective-permute-done.30, pred[]{:T(512)S(6)} %eq.55, ...), kind=kLoop, calls=%fused_computation.12 | loop fusion | flops 4194304 | bytes 10485762 | tf_op jit(solution)/shard_map/jit(_where)/select_n | solution.py:335
  255.0 7.2 %shard_map.35 = (f32[2048,4096]{1,0:T(8,128)}, f32[8,128]{1,0:T(8,128)}) custom-call(s32[2]{0:T(128)S(1)} %pad_add_fusion.5.blocks_ref, s32[1]{0:T(128)} %bitcast.2.place_ref, bf16[2048,2048]{1,0:T(8,128)(2,1)S(1)} %copy-done.4, bf16[2048,256]{1,0:T(8,128)(2,1)S(1)} %get-tuple-element.249.refs_0_, ...), custom_call_target="tpu_custom_call", output_to_operand_aliasing={{0}: (5, {})} | custom-call | flops 4294967296 | bytes 14680064 | tf_op jit(solution)/shard_map/pallas_call | solution.py:175
  262.2 7.2 %shard_map.36 = (f32[2048,4096]{1,0:T(8,128)}, f32[8,128]{1,0:T(8,128)}) custom-call(s32[2]{0:T(128)S(1)} %pad_add_fusion.4.blocks_ref, s32[1]{0:T(128)} %bitcast.2.place_ref, bf16[2048,2048]{1,0:T(8,128)(2,1)S(1)} %copy-done.4, bf16[2048,256]{1,0:T(8,128)(2,1)S(1)} %get-tuple-element.287.refs_0_, ...), custom_call_target="tpu_custom_call", output_to_operand_aliasing={{0}: (5, {})} | custom-call | flops 4294967296 | bytes 14680064 | tf_op jit(solution)/shard_map/pallas_call | solution.py:175
  269.4 8.7 %shard_map.37 = (f32[2048,4096]{1,0:T(8,128)}, f32[8,128]{1,0:T(8,128)}) custom-call(s32[2]{0:T(128)S(1)} %pad_add_fusion.blocks_ref, s32[1]{0:T(128)} %bitcast.2.place_ref, bf16[2048,2048]{1,0:T(8,128)(2,1)S(1)} %copy-done.4, bf16[2048,256]{1,0:T(8,128)(2,1)} %collective-permute-done.36.refs_0_, ...), custom_call_target="tpu_custom_call", output_to_operand_aliasing={{0}: (5, {})} | custom-call | flops 4294967296 | bytes 14680064 | tf_op jit(solution)/shard_map/pallas_call | solution.py:175
  (130 shorter events, 113.0 us)
Async XLA Ops:
  2.7 24.2 %collective-permute-start = (bf16[2048,256]{1,0:T(8,128)(2,1)S(1)}, bf16[2048,256]{1,0:T(8,128)(2,1)}, u32[]{:S(2)}, u32[]{:S(2)}) collective-permute-start(bf16[2048,256]{1,0:T(8,128)(2,1)S(1)} %get-tuple-element.152.refs_0_), channel_id=1, source_target_pairs={{0,8},{1,9},{2,10},{3,11},{4,12},{5,13},{6,14},{7,15},{8,0},{9,1},... | collective-permute-start | bytes 3145736 | tf_op jit(solution)/shard_map/ppermute | solution.py:237
  4.1 25.7 %collective-permute-start.1 = (bf16[2048,256]{1,0:T(8,128)(2,1)S(1)}, bf16[2048,256]{1,0:T(8,128)(2,1)}, u32[]{:S(2)}, u32[]{:S(2)}) collective-permute-start(bf16[2048,256]{1,0:T(8,128)(2,1)S(1)} %get-tuple-element.152.refs_0_), channel_id=1, source_target_pairs={{8,16},{9,17},{10,18},{11,19},{12,20},{13,21},{14,22},{15,23},{16,... | collective-permute-start | bytes 3145736 | tf_op jit(solution)/shard_map/ppermute | solution.py:237
  6.0 23.9 %collective-permute-start.2 = (bf16[2048,256]{1,0:T(8,128)(2,1)S(1)}, bf16[2048,256]{1,0:T(8,128)(2,1)S(1)}, u32[]{:S(2)}, u32[]{:S(2)}) collective-permute-start(bf16[2048,256]{1,0:T(8,128)(2,1)S(1)} %get-tuple-element.152.refs_0_), channel_id=1, source_target_pairs={{0,4},{1,5},{2,6},{3,7},{4,0},{5,1},{6,2},{7,3},{8,12},{9,13},{10,... | collective-permute-start | bytes 3145736 | tf_op jit(solution)/shard_map/ppermute | solution.py:237
  7.3 23.5 %collective-permute-start.3 = (bf16[2048,256]{1,0:T(8,128)(2,1)S(1)}, bf16[2048,256]{1,0:T(8,128)(2,1)S(1)}, u32[]{:S(2)}, u32[]{:S(2)}) collective-permute-start(bf16[2048,256]{1,0:T(8,128)(2,1)S(1)} %get-tuple-element.152.refs_0_), channel_id=1, source_target_pairs={{0,2},{1,3},{2,0},{3,1},{4,6},{5,7},{6,4},{7,5},{8,10},{9,11},{10,... | collective-permute-start | bytes 3145736 | tf_op jit(solution)/shard_map/ppermute | solution.py:237
  8.5 22.3 %collective-permute-start.4 = (bf16[2048,256]{1,0:T(8,128)(2,1)S(1)}, bf16[2048,256]{1,0:T(8,128)(2,1)S(1)}, u32[]{:S(2)}, u32[]{:S(2)}) collective-permute-start(bf16[2048,256]{1,0:T(8,128)(2,1)S(1)} %get-tuple-element.152.refs_0_), channel_id=1, source_target_pairs={{0,1},{1,0},{2,3},{3,2},{4,5},{5,4},{6,7},{7,6},{8,9},{9,8},{10,11... | collective-permute-start | bytes 3145736 | tf_op jit(solution)/shard_map/ppermute | solution.py:237
  31.9 22.2 %collective-permute-start.5 = (bf16[2048,256]{1,0:T(8,128)(2,1)}, bf16[2048,256]{1,0:T(8,128)(2,1)}, u32[]{:S(2)}, u32[]{:S(2)}) collective-permute-start(bf16[2048,256]{1,0:T(8,128)(2,1)} %collective-permute-done.1), channel_id=1, source_target_pairs={{8,0},{9,1},{10,2},{11,3},{12,4},{13,5},{14,6},{15,7},{16,24},{17,... | collective-permute-start | bytes 3145736 | tf_op jit(solution)/shard_map/ppermute | solution.py:237
  34.5 24.4 %collective-permute-start.6 = (bf16[2048,256]{1,0:T(8,128)(2,1)}, bf16[2048,256]{1,0:T(8,128)(2,1)}, u32[]{:S(2)}, u32[]{:S(2)}) collective-permute-start(bf16[2048,256]{1,0:T(8,128)(2,1)} %collective-permute-done), channel_id=1, source_target_pairs={{8,16},{9,17},{10,18},{11,19},{12,20},{13,21},{14,22},{15,23},{16,... | collective-permute-start | bytes 3145736 | tf_op jit(solution)/shard_map/ppermute | solution.py:237
  37.1 22.1 %collective-permute-start.7 = (bf16[2048,256]{1,0:T(8,128)(2,1)S(1)}, bf16[2048,256]{1,0:T(8,128)(2,1)}, u32[]{:S(2)}, u32[]{:S(2)}) collective-permute-start(bf16[2048,256]{1,0:T(8,128)(2,1)S(1)} %get-tuple-element.211.refs_1_), channel_id=1, source_target_pairs={{0,4},{1,5},{2,6},{3,7},{4,0},{5,1},{6,2},{7,3},{8,12},{9,13},{10,... | collective-permute-start | bytes 3145736 | tf_op jit(solution)/shard_map/ppermute | solution.py:237
  37.6 21.7 %collective-permute-start.8 = (bf16[2048,256]{1,0:T(8,128)(2,1)S(1)}, bf16[2048,256]{1,0:T(8,128)(2,1)S(1)}, u32[]{:S(2)}, u32[]{:S(2)}) collective-permute-start(bf16[2048,256]{1,0:T(8,128)(2,1)S(1)} %get-tuple-element.211.refs_1_), channel_id=1, source_target_pairs={{0,2},{1,3},{2,0},{3,1},{4,6},{5,7},{6,4},{7,5},{8,10},{9,11},{10,... | collective-permute-start | bytes 3145736 | tf_op jit(solution)/shard_map/ppermute | solution.py:237
  61.6 22.8 %collective-permute-start.11 = (bf16[2048,256]{1,0:T(8,128)(2,1)S(1)}, bf16[2048,256]{1,0:T(8,128)(2,1)}, u32[]{:S(2)}, u32[]{:S(2)}) collective-permute-start(bf16[2048,256]{1,0:T(8,128)(2,1)S(1)} %get-tuple-element.211.refs_1_), channel_id=1, source_target_pairs={{8,16},{9,17},{10,18},{11,19},{12,20},{13,21},{14,22},{15,23},{16,... | collective-permute-start | bytes 3145736 | tf_op jit(solution)/shard_map/ppermute | solution.py:237
  67.3 20.8 %collective-permute-start.12 = (bf16[2048,256]{1,0:T(8,128)(2,1)}, bf16[2048,256]{1,0:T(8,128)(2,1)}, u32[]{:S(2)}, u32[]{:S(2)}) collective-permute-start(bf16[2048,256]{1,0:T(8,128)(2,1)} %get-tuple-element.272), channel_id=1, source_target_pairs={{0,4},{1,5},{2,6},{3,7},{4,0},{5,1},{6,2},{7,3},{8,12},{9,13},{10,... | collective-permute-start | bytes 3145736 | tf_op jit(solution)/shard_map/ppermute | solution.py:237
  68.5 20.6 %collective-permute-start.13 = (bf16[2048,256]{1,0:T(8,128)(2,1)}, bf16[2048,256]{1,0:T(8,128)(2,1)}, u32[]{:S(2)}, u32[]{:S(2)}) collective-permute-start(bf16[2048,256]{1,0:T(8,128)(2,1)} %get-tuple-element.271), channel_id=1, source_target_pairs={{0,2},{1,3},{2,0},{3,1},{4,6},{5,7},{6,4},{7,5},{8,10},{9,11},{10,... | collective-permute-start | bytes 3145736 | tf_op jit(solution)/shard_map/ppermute | solution.py:237
  114.4 23.5 %collective-permute-start.20 = (bf16[2048,256]{1,0:T(8,128)(2,1)}, bf16[2048,256]{1,0:T(8,128)(2,1)S(1)}, u32[]{:S(2)}, u32[]{:S(2)}) collective-permute-start(bf16[2048,256]{1,0:T(8,128)(2,1)} %collective-permute-done.11), channel_id=1, source_target_pairs={{8,0},{9,1},{10,2},{11,3},{12,4},{13,5},{14,6},{15,7},{16,24},{17,... | collective-permute-start | bytes 3145736 | tf_op jit(solution)/shard_map/ppermute | solution.py:237
  143.3 38.4 %collective-permute-start.25 = (bf16[2048,256]{1,0:T(8,128)(2,1)}, bf16[2048,256]{1,0:T(8,128)(2,1)}, u32[]{:S(2)}, u32[]{:S(2)}) collective-permute-start(bf16[2048,256]{1,0:T(8,128)(2,1)} %collective-permute-done.21), channel_id=1, source_target_pairs={{8,0},{9,1},{10,2},{11,3},{12,4},{13,5},{14,6},{15,7},{16,24},{17,... | collective-permute-start | bytes 3145736 | tf_op jit(solution)/shard_map/ppermute | solution.py:237
  148.5 33.2 %collective-permute-start.26 = (bf16[2048,256]{1,0:T(8,128)(2,1)}, bf16[2048,256]{1,0:T(8,128)(2,1)}, u32[]{:S(2)}, u32[]{:S(2)}) collective-permute-start(bf16[2048,256]{1,0:T(8,128)(2,1)} %get-tuple-element.270), channel_id=1, source_target_pairs={{0,4},{1,5},{2,6},{3,7},{4,0},{5,1},{6,2},{7,3},{8,12},{9,13},{10,... | collective-permute-start | bytes 3145736 | tf_op jit(solution)/shard_map/ppermute | solution.py:237
  148.8 32.9 %collective-permute-start.27 = (bf16[2048,256]{1,0:T(8,128)(2,1)}, bf16[2048,256]{1,0:T(8,128)(2,1)}, u32[]{:S(2)}, u32[]{:S(2)}) collective-permute-start(bf16[2048,256]{1,0:T(8,128)(2,1)} %get-tuple-element.269), channel_id=1, source_target_pairs={{0,2},{1,3},{2,0},{3,1},{4,6},{5,7},{6,4},{7,5},{8,10},{9,11},{10,... | collective-permute-start | bytes 3145736 | tf_op jit(solution)/shard_map/ppermute | solution.py:237
  152.5 29.3 %collective-permute-start.28 = (bf16[2048,256]{1,0:T(8,128)(2,1)}, bf16[2048,256]{1,0:T(8,128)(2,1)}, u32[]{:S(2)}, u32[]{:S(2)}) collective-permute-start(bf16[2048,256]{1,0:T(8,128)(2,1)} %get-tuple-element.292), channel_id=1, source_target_pairs={{0,1},{1,0},{2,3},{3,2},{4,5},{5,4},{6,7},{7,6},{8,9},{9,8},{10,11... | collective-permute-start | bytes 3145736 | tf_op jit(solution)/shard_map/ppermute | solution.py:237
  188.0 24.6 %collective-permute-start.30 = (bf16[2048,256]{1,0:T(8,128)(2,1)}, bf16[2048,256]{1,0:T(8,128)(2,1)}, u32[]{:S(2)}, u32[]{:S(2)}) collective-permute-start(bf16[2048,256]{1,0:T(8,128)(2,1)} %get-tuple-element.290), channel_id=1, source_target_pairs={{0,4},{1,5},{2,6},{3,7},{4,0},{5,1},{6,2},{7,3},{8,12},{9,13},{10,... | collective-permute-start | bytes 3145736 | tf_op jit(solution)/shard_map/ppermute | solution.py:237
  189.3 24.3 %collective-permute-start.31 = (bf16[2048,256]{1,0:T(8,128)(2,1)}, bf16[2048,256]{1,0:T(8,128)(2,1)}, u32[]{:S(2)}, u32[]{:S(2)}) collective-permute-start(bf16[2048,256]{1,0:T(8,128)(2,1)} %get-tuple-element.283), channel_id=1, source_target_pairs={{0,2},{1,3},{2,0},{3,1},{4,6},{5,7},{6,4},{7,5},{8,10},{9,11},{10,... | collective-permute-start | bytes 3145736 | tf_op jit(solution)/shard_map/ppermute | solution.py:237
  189.5 24.1 %collective-permute-start.32 = (bf16[2048,256]{1,0:T(8,128)(2,1)}, bf16[2048,256]{1,0:T(8,128)(2,1)}, u32[]{:S(2)}, u32[]{:S(2)}) collective-permute-start(bf16[2048,256]{1,0:T(8,128)(2,1)} %get-tuple-element.259), channel_id=1, source_target_pairs={{0,1},{1,0},{2,3},{3,2},{4,5},{5,4},{6,7},{7,6},{8,9},{9,8},{10,11... | collective-permute-start | bytes 3145736 | tf_op jit(solution)/shard_map/ppermute | solution.py:237
  217.1 23.4 %collective-permute-start.33 = (bf16[2048,256]{1,0:T(8,128)(2,1)}, bf16[2048,256]{1,0:T(8,128)(2,1)}, u32[]{:S(2)}, u32[]{:S(2)}) collective-permute-start(bf16[2048,256]{1,0:T(8,128)(2,1)} %get-tuple-element.289), channel_id=1, source_target_pairs={{0,4},{1,5},{2,6},{3,7},{4,0},{5,1},{6,2},{7,3},{8,12},{9,13},{10,... | collective-permute-start | bytes 3145736 | tf_op jit(solution)/shard_map/ppermute | solution.py:237
  217.4 25.2 %collective-permute-start.34 = (bf16[2048,256]{1,0:T(8,128)(2,1)}, bf16[2048,256]{1,0:T(8,128)(2,1)}, u32[]{:S(2)}, u32[]{:S(2)}) collective-permute-start(bf16[2048,256]{1,0:T(8,128)(2,1)} %collective-permute-done.30), channel_id=1, source_target_pairs={{0,2},{1,3},{4,6},{5,7},{8,10},{9,11},{12,14},{13,15},{18,16},{19,... | collective-permute-start | bytes 3145736 | tf_op jit(solution)/shard_map/ppermute | solution.py:237
  218.9 23.7 %collective-permute-start.35 = (bf16[2048,256]{1,0:T(8,128)(2,1)}, bf16[2048,256]{1,0:T(8,128)(2,1)S(1)}, u32[]{:S(2)}, u32[]{:S(2)}) collective-permute-start(bf16[2048,256]{1,0:T(8,128)(2,1)} %get-tuple-element.275), channel_id=1, source_target_pairs={{0,1},{1,0},{2,3},{3,2},{4,5},{5,4},{6,7},{7,6},{8,9},{9,8},{10,11... | collective-permute-start | bytes 3145736 | tf_op jit(solution)/shard_map/ppermute | solution.py:237
  247.6 21.8 %collective-permute-start.36 = (bf16[2048,256]{1,0:T(8,128)(2,1)}, bf16[2048,256]{1,0:T(8,128)(2,1)}, u32[]{:S(2)}, u32[]{:S(2)}) collective-permute-start(bf16[2048,256]{1,0:T(8,128)(2,1)} %get-tuple-element.288), channel_id=1, source_target_pairs={{0,1},{1,0},{2,3},{3,2},{4,5},{5,4},{6,7},{7,6},{8,9},{9,8},{10,11... | collective-permute-start | bytes 3145736 | tf_op jit(solution)/shard_map/ppermute | solution.py:237
  (39 other events, 483.0 us)
where the time goes:
time: 280 us; the launch traced here: 278 us
  waiting for transfers between devices  80.3 us (29%)
  starting transfers between devices  72.9 us (26%)
  Pallas kernels  66.3 us (24%)
  other arithmetic  33.7 us (12%)
  local copies, waits for them, and re-layouts  24.6 us (9%)
    ppermute x38, waiting for transfers between devices, send(): running.append((name, lax.ppermute(value, AXES, lay.moves(target))))  80.3 us
    ppermute x38, starting transfers between devices, send(): running.append((name, lax.ppermute(value, AXES, lay.moves(target))))  72.9 us
    pallas_call x6, Pallas kernels, multiply(): pl.pallas_call(kernel, grid_spec=pltpu.PrefetchScalarGridSpec(num_scalar_...  56.9 us
    unnamed x50, local copies, waits for them, and re-layouts  23.9 us
    select_n x6, other arithmetic, swap(): send(('swapped', h, s, m), jnp.where(first_kept, two, one), to_mate)  19 us
    pallas_call x4, Pallas kernels, turn(): pl.pallas_call(kernel, grid=(depth // TURN,), in_specs=in_specs, out_spec...  9.41 us
    select_n x2, other arithmetic, give_more(): value = jnp.where(off == m, got['own_x', h, 1], second(h, off ^ m))  6.21 us
    select_n x2, other arithmetic, give(): value = jnp.where(off == m, got['pair', h], first(h, off ^ m))  6.07 us
  transfers between devices with their start and end apart: 38, of which 21 were waited for; matrix products, arithmetic and copies ran while one was open for 6% of the time, Pallas kernels for 21%

commit v1 on v0

--- a/solution.py
+++ b/solution.py
@@ -72,10 +72,6 @@
 
 def to_outer(z, x, y, c):
     return (z ^ 1, x, y, c) if inner(z) else None
-
-
-def to_back(z, x, y, c):
-    return (z, x, y ^ 1, c) if apart(z, y) == 0 else None
 
 
 def to_far(q):
@@ -126,15 +122,28 @@
     )(*operands)
 
 
-def multiply(tile, rows, chunks, blocks, place, shape, band):
+def multiply(tile, rows, columns, blocks, place, shape, band):
     high, depth = rows.shape
-    step, count = chunks[0].shape[1], len(chunks)
+    step, count = columns[0][0][0].shape[1], len(columns)
     bands = high // band
-
-    def kernel(blocks_ref, place_ref, rows_ref, *refs):
-        chunk_refs = refs[:count]
-        tile_ref, token_ref, result, sems = refs[-4:]
+    options = [arrays for arrays, _ in columns]
+    picks = [jnp.asarray(pick, jnp.int32) for _, pick in columns]
+    flat = sum(options, [])
+
+    def kernel(blocks_ref, place_ref, picks_ref, rows_ref, *refs):
+        tile_ref, token_ref, right, result, in_sems, out_sems = refs[-6:]
         i = pl.program_id(0)
+
+        def fetch(act):
+            at = 0
+            for k, arrays in enumerate(options):
+                for n in range(len(arrays)):
+
+                    @pl.when(picks_ref[k] == n)
+                    def _(k=k, source=refs[at + n]):
+                        act(pltpu.make_async_copy(source, right.at[:, k * step : (k + 1) * step], in_sems.at[k]))
+
+                at += len(arrays)
 
         def copies(i):
             at = pl.multiple_of((i ^ place_ref[0]) * band, band)
@@ -142,18 +151,22 @@
                 pltpu.make_async_copy(
                     result.at[i % 2, :, k * step : (k + 1) * step],
                     tile_ref.at[pl.ds(at, band), pl.ds(pl.multiple_of(blocks_ref[k] * step, step), step)],
-                    sems.at[i % 2, k],
+                    out_sems.at[i % 2, k],
                 )
                 for k in range(count)
             ]
+
+        @pl.when(i == 0)
+        def _():
+            fetch(lambda copy: copy.start())
+            fetch(lambda copy: copy.wait())
 
         @pl.when(i >= 2)
         def _():
             for copy in copies(i - 2):
                 copy.wait()
 
-        right = jnp.concatenate([ref[...] for ref in chunk_refs], axis=1)
-        result[i % 2] = jnp.dot(rows_ref[...], right, preferred_element_type=jnp.float32)
+        result[i % 2] = jnp.dot(rows_ref[...], right[...], preferred_element_type=jnp.float32)
         for copy in copies(i):
             copy.start()
 
@@ -164,26 +177,28 @@
                 for copy in copies(last):
                     copy.wait()
 
-    operands = [rows, *chunks]
-    in_specs = [pl.BlockSpec((band, depth), lambda i, b, p: (i, 0))]
-    in_specs += [pl.BlockSpec((depth, step), lambda i, b, p: (0, 0)) for _ in chunks]
+    operands = [rows, *flat]
+    in_specs = [pl.BlockSpec((band, depth), lambda i, b, p, k: (i, 0))]
+    in_specs += [pl.BlockSpec(memory_space=pl.ANY) for _ in flat]
     aliases = {}
     if tile is not None:
         operands.append(tile)
         in_specs.append(pl.BlockSpec(memory_space=pl.ANY))
-        aliases = {len(operands) + 1: 0}
+        aliases = {len(operands) + 2: 0}
     return pl.pallas_call(
         kernel,
         grid_spec=pltpu.PrefetchScalarGridSpec(
-            num_scalar_prefetch=2,
+            num_scalar_prefetch=3,
             grid=(bands,),
             in_specs=in_specs,
             out_specs=[
                 pl.BlockSpec(memory_space=pl.ANY),
-                pl.BlockSpec((8, LANES), lambda i, b, p: (0, 0)),
+                pl.BlockSpec((8, LANES), lambda i, b, p, k: (0, 0)),
             ],
             scratch_shapes=[
+                pltpu.VMEM((depth, step * count), jnp.bfloat16),
                 pltpu.VMEM((2, band, step * count), jnp.float32),
+                pltpu.SemaphoreType.DMA((count,)),
                 pltpu.SemaphoreType.DMA((2, count)),
             ],
         ),
@@ -198,7 +213,7 @@
             bytes_accessed=2 * high * depth + (2 * depth + 4 * high) * step * count,
             transcendentals=0,
         ),
-    )(jnp.stack(blocks), place[None], *operands)
+    )(jnp.stack(blocks), place[None], jnp.stack(picks), *operands)
 
 
 def solution(mesh):
@@ -259,6 +274,15 @@
             for m in others:
                 send(("row", h, m), got["own", h], along_y(m))
 
+        def row_of(core, h):
+            for m in others:
+                who = lambda z, x, y, c, m=m: (z, x, y ^ m, c) if c == core else None
+                send(("row_of", h, m, core), got["own", h], who)
+
+        def join_rows(h):
+            for m in others:
+                got["row", h, m] = jnp.where(c == 0, got["row_of", h, m, 0], got["row_of", h, m, 1])
+
         def give(h):
             for m in others:
                 value = jnp.where(off == m, got["pair", h], first(h, off ^ m))
@@ -297,7 +321,7 @@
 
         def back(h):
             for s in shifts:
-                send(("back", h, s), got["give_x", h, s, 1], to_back)
+                send(("back", h, s), got["give_x", h, s, 1], along_y(1))
 
 
         def mate(kind, h):
@@ -308,31 +332,36 @@
             return [(s, m) for s in (shifts if "x" in kind else (0,)) for m in (others if "y" in kind else (0,))]
 
         def both(h, s, m):
+            away = jnp.where(home, 0, 1)
             if s == 0 and m == 0:
-                return first(h, off), second(h, off)
+                which = jnp.where(beside, jnp.where(is_inner, 1, 2), jnp.where(home, 0, off + 1))
+                sources = []
+                for kind in ("own", "pair"):
+                    names = [(kind, h), (kind + "_cross", h), (kind + "_outer", h)]
+                    names += [("far_" + kind, h, n) for n in halves]
+                    sources.append(([got[n] for n in names], which))
+                return sources
             if s == 0:
-                return (
-                    jnp.where(home, got["row", h, m], got["give", h, m]),
-                    jnp.where(home, got["give", h, m], got["give_more", h, m]),
-                )
+                return ([got["row", h, m], got["give", h, m]], away), ([got["give", h, m], got["give_more", h, m]], away)
             if m == 0:
                 return (
-                    jnp.where(home, got["own_x", h, s], got["near_x", h, s]),
-                    jnp.where(home, got["near_x", h, s], got["more_x", h, s, 1]),
+                    ([got["own_x", h, s], got["near_x", h, s]], away),
+                    ([got["near_x", h, s], got["more_x", h, s, 1]], away),
                 )
-            last = got.get(("rest_x", h, s, m), got["back", h, s])
-            if m == 1 and lay.ys > 2:
-                last = jnp.where(beside, got["back", h, s], last)
-            return (
-                jnp.where(home, got["give_more", h, m], got["give_x", h, s, m]),
-                jnp.where(home, got["more_x", h, s, m], last),
-            )
+            last, which = [got["more_x", h, s, m], got["back", h, s]], away
+            if lay.ys > 2:
+                last.append(got["rest_x", h, s, m])
+                which = jnp.where(home, 0, jnp.where(beside & (m == 1), 1, 2))
+            return ([got["give_more", h, m], got["give_x", h, s, m]], away), (last, which)
+
+        def kept(h, s, m):
+            (one, which_one), (two, which_two) = both(h, s, m)
+            return one + two, jnp.where(first_kept, which_one, len(one) + which_two)
 
         def swap(kind, h):
             for s, m in places(kind):
                 one, two = both(h, s, m)
-                got["kept", h, s, m] = jnp.where(first_kept, one, two)
-                send(("swapped", h, s, m), jnp.where(first_kept, two, one), to_mate)
+                send(("swapped", h, s, m), jnp.where(first_kept, choose(*two), choose(*one)), to_mate)
 
 
         def lay_row(m, side):
@@ -352,7 +381,7 @@
             for kind in kinds:
                 for s, m in places(kind):
                     for side in sides:
-                        chunks.append(got["swapped" if side else "kept", h, s, m])
+                        chunks.append(([got["swapped", h, s, m]], 0) if side else kept(h, s, m))
                         block = ((x - s) % lay.xs * lay.ys + (y ^ m)) * CORES + (c ^ side)
                         blocks.append(block * PARTS + h)
             tile = got.get("tile")
@@ -360,16 +389,19 @@
                 tile = jnp.zeros(shape, jnp.float32) if tile is None else tile
                 for chunk, block in zip(chunks, blocks):
                     dims = (((0,), (0,)), ((), ()))
-                    part = lax.dot_general(got["rows"], chunk, dims, preferred_element_type=jnp.float32)
+                    part = lax.dot_general(got["rows"], choose(*chunk), dims, preferred_element_type=jnp.float32)
                     tile = lax.dynamic_update_slice(tile, part, (0, block * step))
                 got["tile"] = tile
             else:
                 got["tile"], got["mark", "tile"] = multiply(tile, got["rows"], chunks, blocks, narrow_at, shape, width)
 
+        row_of(1, 0)
+        settle()
+
         pair(0)
         cross("own", 0)
         own_x(0)
-        row(0)
+        row_of(0, 0)
         mate("own", 0)
         settle()
 
@@ -384,6 +416,7 @@
         cross("own", 1)
         near_x(0)
         give(0)
+        join_rows(0)
         mate("row", 0)
         lay_row(0, 0)
         settle()
@@ -424,15 +457,15 @@
         back(1)
         swap("y", 1)
         product(1, "")
+        product(1, "y", sides=(0,))
         settle()
 
         swap("x", 1)
         swap("xy", 1)
-        product(1, "y")
         product(1, "x", "xy", sides=(0,))
         settle()
 
-        product(1, "x", "xy", sides=(1,))
+        product(1, "y", "x", "xy", sides=(1,))
         return got["tile"]
 
     placed = (P(None, AXES), P())

time: 280 us -> 268 us (0.957)
  starting transfers between devices: 72.9 us -> 49.7 us
  local copies, waits for them, and re-layouts: 24.6 us -> 44.5 us
  waiting for transfers between devices: 80.3 us -> 67.6 us
  Pallas kernels: 66.3 us -> 72.9 us
    ppermute x38 -> x39, starting transfers between devices: 72.9 us -> 49.7 us  [send(): running.append((name, lax.ppermute(value, AXES, lay.moves(target))))]
    unnamed x50 -> x76, local copies, waits for them, and re-layouts: 23.9 us -> 43.8 us
    ppermute x38 -> x39, waiting for transfers between devices: 80.3 us -> 67.6 us  [send(): running.append((name, lax.ppermute(value, AXES, lay.moves(target))))]
    pallas_call x6, Pallas kernels: 56.9 us -> 61.3 us  [multiply(): pl.pallas_call(kernel, grid_spec=pltpu.PrefetchScalarGridSpec(num_scalar_...]
    select_n x8 -> x7, other arithmetic: 25.2 us -> 23 us  [the longest x6 20.7 us: swap(): jnp.where(first_kept, choose(*two), choose(*one))]
  transfers between devices with their start and end apart: 38 -> 39, of which waited for: 21 -> 20; matrix products, arithmetic and copies ran while one was open for 6% -> 7% of each run, Pallas kernels for 21% -> 23%
where the time goes in v1:
time: 268 us; the launch traced here: 267 us
  Pallas kernels  72.9 us (27%)
  waiting for transfers between devices  67.6 us (25%)
  starting transfers between devices  49.7 us (19%)
  local copies, waits for them, and re-layouts  44.5 us (17%)
  other arithmetic  31.4 us (12%)
    ppermute x39, waiting for transfers between devices, send(): running.append((name, lax.ppermute(value, AXES, lay.moves(target))))  67.6 us
    pallas_call x6, Pallas kernels, multiply(): pl.pallas_call(kernel, grid_spec=pltpu.PrefetchScalarGridSpec(num_scalar_...  61.3 us
    ppermute x39, starting transfers between devices, send(): running.append((name, lax.ppermute(value, AXES, lay.moves(target))))  49.7 us
    unnamed x76, local copies, waits for them, and re-layouts  43.8 us
    select_n x6, other arithmetic, swap(): jnp.where(first_kept, choose(*two), choose(*one))  20.7 us
    pallas_call x4, Pallas kernels, turn(): pl.pallas_call(kernel, grid=(depth // TURN,), in_specs=in_specs, out_spec...  11.6 us
    select_n x2, other arithmetic, give(): value = jnp.where(off == m, got['pair', h], first(h, off ^ m))  5.95 us
  transfers between devices with their start and end apart: 39, of which 20 were waited for; matrix products, arithmetic and copies ran while one was open for 7% of the time, Pallas kernels for 23%

profile of v1, /device:TPU:17, one launch (start us, length us, event | category | flops | bytes accessed | tf_op | source)
XLA Modules:
  0.0 266.6 jit_solution(3637856466642614160)
XLA Ops:
  5.9 16.9 %collective-permute-done = bf16[2048,256]{1,0:T(8,128)(2,1)S(1)} collective-permute-done((bf16[2048,256]{1,0:T(8,128)(2,1)S(1)}, bf16[2048,256]{1,0:T(8,128)(2,1)S(1)}, u32[]{:S(2)}, u32[]{:S(2)}) %collective-permute-start) | collective-permute-done | bytes 1048608 | tf_op jit(solution)/shard_map/ppermute | solution.py:252
  29.9 7.3 %collective-permute-done.1.refs_3_ = bf16[2048,256]{1,0:T(8,128)(2,1)} collective-permute-done((bf16[2048,256]{1,0:T(8,128)(2,1)S(1)}, bf16[2048,256]{1,0:T(8,128)(2,1)}, u32[]{:S(2)}, u32[]{:S(2)}) %collective-permute-start.1) | collective-permute-done | bytes 1048608 | tf_op jit(solution)/shard_map/ppermute | solution.py:252
  42.3 6.4 %collective-permute-start.6 = (bf16[2048,256]{1,0:T(8,128)(2,1)}, bf16[2048,256]{1,0:T(8,128)(2,1)}, u32[]{:S(2)}, u32[]{:S(2)}) collective-permute-start(bf16[2048,256]{1,0:T(8,128)(2,1)} %collective-permute-done.2.refs_1_), channel_id=1, source_target_pairs={{8,0},{9,1},{10,2},{11,3},{12,4},{13,5},{14,6},{15,7},{16,24},{17,... | collective-permute-start | bytes 3145736 | tf_op jit(solution)/shard_map/ppermute | solution.py:252
  54.3 6.3 %collective-permute-done.6.refs_2_ = bf16[2048,256]{1,0:T(8,128)(2,1)} collective-permute-done((bf16[2048,256]{1,0:T(8,128)(2,1)}, bf16[2048,256]{1,0:T(8,128)(2,1)}, u32[]{:S(2)}, u32[]{:S(2)}) %collective-permute-start.6) | collective-permute-done | bytes 1048608 | tf_op jit(solution)/shard_map/ppermute | solution.py:252
  60.5 5.7 %collective-permute-done.7.refs_4_ = bf16[2048,256]{1,0:T(8,128)(2,1)} collective-permute-done((bf16[2048,256]{1,0:T(8,128)(2,1)}, bf16[2048,256]{1,0:T(8,128)(2,1)}, u32[]{:S(2)}, u32[]{:S(2)}) %collective-permute-start.7) | collective-permute-done | bytes 1048608 | tf_op jit(solution)/shard_map/ppermute | solution.py:252
  81.8 3.4 %copy-done = bf16[2048,2048]{1,0:T(8,128)(2,1)} copy-done((bf16[2048,2048]{1,0:T(8,128)(2,1)}, bf16[2048,2048]{1,0:T(8,128)(2,1)S(1)}, u32[]{:S(2)}) %copy-start) | copy-done | bytes 8388632
  87.7 4.4 %collective-permute-done.13.refs_1_.refs_2_ = bf16[2048,256]{1,0:T(8,128)(2,1)} collective-permute-done((bf16[2048,256]{1,0:T(8,128)(2,1)}, bf16[2048,256]{1,0:T(8,128)(2,1)}, u32[]{:S(2)}, u32[]{:S(2)}) %collective-permute-start.13) | collective-permute-done | bytes 1048608 | tf_op jit(solution)/shard_map/ppermute | solution.py:252
  92.5 5.0 %select_select_fusion.12 = (bf16[2048,256]{1,0:T(8,128)(2,1)}, bf16[2048,256]{1,0:T(8,128)(2,1)}, bf16[2048,256]{1,0:T(8,128)(2,1)}) fusion(bf16[2048,256]{1,0:T(8,128)(2,1)} %collective-permute-done.6.refs_2_, bf16[2048,256]{1,0:T(8,128)(2,1)} %collective-permute-done.2.refs_1_, bf16[2048,256]{1,0:T(8,128)(2,1)S(1)} %get-tuple-element.218.refs_0_, ...), kind=kLoop, calls=%fused_computation.14 | loop fusion | flops 4718592 | bytes 11534343 | tf_op jit(solution)/shard_map/jit(_where)/select_n | solution.py:364
  107.2 3.4 %copy-done.2 = bf16[2048,2048]{1,0:T(8,128)(2,1)} copy-done((bf16[2048,2048]{1,0:T(8,128)(2,1)}, bf16[2048,2048]{1,0:T(8,128)(2,1)S(1)}, u32[]{:S(2)}) %copy-start.2) | copy-done | bytes 8388632
  111.1 5.3 %collective-permute-done.17.refs_6_ = bf16[2048,256]{1,0:T(8,128)(2,1)} collective-permute-done((bf16[2048,256]{1,0:T(8,128)(2,1)}, bf16[2048,256]{1,0:T(8,128)(2,1)}, u32[]{:S(2)}, u32[]{:S(2)}) %collective-permute-start.17) | collective-permute-done | bytes 1048608 | tf_op jit(solution)/shard_map/ppermute | solution.py:252
  117.3 4.0 %collective-permute-start.21 = (bf16[2048,256]{1,0:T(8,128)(2,1)}, bf16[2048,256]{1,0:T(8,128)(2,1)S(1)}, u32[]{:S(2)}, u32[]{:S(2)}) collective-permute-start(bf16[2048,256]{1,0:T(8,128)(2,1)} %collective-permute-done.12.refs_1_), channel_id=1, source_target_pairs={{8,0},{9,1},{10,2},{11,3},{12,4},{13,5},{14,6},{15,7},{16,24},{17,... | collective-permute-start | bytes 3145736 | tf_op jit(solution)/shard_map/ppermute | solution.py:252
  131.3 3.5 %shard_map.31 = (bf16[2048,2048]{1,0:T(8,128)(2,1)S(1)}, f32[8,128]{1,0:T(8,128)}) custom-call(bf16[2048,256]{1,0:T(8,128)(2,1)} %collective-permute-done.15.refs_0_, bf16[2048,256]{1,0:T(8,128)(2,1)} %collective-permute-done.19.refs_1_, bf16[2048,2048]{1,0:T(8,128)(2,1)S(1)} %get-tuple-element.208.refs_2_), custom_call_target="tpu_custom_call", output_to_operand_aliasing={{0}: (2, {})} | custom-call | bytes 4194304 | tf_op jit(solution)/shard_map/pallas_call | solution.py:105
  139.1 4.1 %collective-permute-done.22.refs_4_ = bf16[2048,256]{1,0:T(8,128)(2,1)} collective-permute-done((bf16[2048,256]{1,0:T(8,128)(2,1)S(1)}, bf16[2048,256]{1,0:T(8,128)(2,1)}, u32[]{:S(2)}, u32[]{:S(2)}) %collective-permute-start.22) | collective-permute-done | bytes 1048608 | tf_op jit(solution)/shard_map/ppermute | solution.py:252
  158.4 3.4 %copy-done.5 = bf16[2048,2048]{1,0:T(8,128)(2,1)S(1)} copy-done((bf16[2048,2048]{1,0:T(8,128)(2,1)S(1)}, bf16[2048,2048]{1,0:T(8,128)(2,1)}, u32[]{:S(2)}) %copy-start.5) | copy-done | bytes 8388632
  165.4 13.9 %shard_map.32 = (f32[2048,4096]{1,0:T(8,128)}, f32[8,128]{1,0:T(8,128)}) custom-call(s32[4]{0:T(128)S(1)} %pad_add_fusion.5.blocks_ref, s32[1]{0:T(128)} %bitcast.3.place_ref, s32[4]{0:T(128)S(1)} %get-tuple-element.318.picks_ref, bf16[2048,2048]{1,0:T(8,128)(2,1)S(1)} %copy-done.5, bf16[2048,256]{1,0:T(8,128)(2,1)S(1)} %copy-done.14, ...), custom_call_target="tpu_custom_call" | custom-call | flops 8589934592 | bytes 20971520 | tf_op jit(solution)/shard_map/pallas_call | solution.py:188
  179.5 4.1 %select_select_fusion.4 = (bf16[2048,256]{1,0:T(8,128)(2,1)}, bf16[2048,256]{1,0:T(8,128)(2,1)}, bf16[2048,256]{1,0:T(8,128)(2,1)}) fusion(bf16[2048,256]{1,0:T(8,128)(2,1)S(1)} %copy-done.28, bf16[2048,256]{1,0:T(8,128)(2,1)} %collective-permute-done.12.refs_1_, bf16[2048,256]{1,0:T(8,128)(2,1)S(1)} %get-tuple-element.264.refs_1_.refs_0_, ...), kind=kLoop, calls=%fused_computation.6 | loop fusion | flops 4718592 | bytes 11534343 | tf_op jit(solution)/shard_map/jit(_where)/select_n | solution.py:364
  185.2 3.4 %copy-done.6 = bf16[2048,2048]{1,0:T(8,128)(2,1)S(1)} copy-done((bf16[2048,2048]{1,0:T(8,128)(2,1)S(1)}, bf16[2048,2048]{1,0:T(8,128)(2,1)}, u32[]{:S(2)}) %copy-start.6) | copy-done | bytes 8388632
  193.5 14.1 %shard_map.33 = (f32[2048,4096]{1,0:T(8,128)}, f32[8,128]{1,0:T(8,128)}) custom-call(s32[4]{0:T(128)S(1)} %pad_add_fusion.6.blocks_ref, s32[1]{0:T(128)} %bitcast.3.place_ref, s32[4]{0:T(128)S(1)} %get-tuple-element.317.picks_ref, bf16[2048,2048]{1,0:T(8,128)(2,1)S(1)} %copy-done.6, ...), custom_call_target="tpu_custom_call", output_to_operand_aliasing={{0}: (14, {})} | custom-call | flops 8589934592 | bytes 20971520 | tf_op jit(solution)/shard_map/pallas_call | solution.py:188
  220.5 8.7 %shard_map.34 = (f32[2048,4096]{1,0:T(8,128)}, f32[8,128]{1,0:T(8,128)}) custom-call(s32[2]{0:T(128)S(1)} %get-tuple-element.319.blocks_ref, s32[1]{0:T(128)} %bitcast.3.place_ref, s32[2]{0:T(128)S(1)} %get-tuple-element.320.picks_ref, bf16[2048,2048]{1,0:T(8,128)(2,1)S(1)} %copy-done.7, ...), custom_call_target="tpu_custom_call", output_to_operand_aliasing={{0}: (11, {})} | custom-call | flops 4294967296 | bytes 14680064 | tf_op jit(solution)/shard_map/pallas_call | solution.py:188
  232.6 4.5 %shard_map.35 = (f32[2048,4096]{1,0:T(8,128)}, f32[8,128]{1,0:T(8,128)}) custom-call(s32[1]{0:T(128)} %bitcast.14.blocks_ref, s32[1]{0:T(128)} %bitcast.3.place_ref, s32[1]{0:T(128)} %bitcast.9.picks_ref, bf16[2048,2048]{1,0:T(8,128)(2,1)S(1)} %copy-done.8, ...), custom_call_target="tpu_custom_call", output_to_operand_aliasing={{0}: (8, {})} | custom-call | flops 2147483648 | bytes 11534336 | tf_op jit(solution)/shard_map/pallas_call | solution.py:188
  237.2 3.8 %select_select_fusion = (bf16[2048,256]{1,0:T(8,128)(2,1)}, bf16[2048,256]{1,0:T(8,128)(2,1)}) fusion(bf16[2048,256]{1,0:T(8,128)(2,1)} %collective-permute-done.31.refs_5_, bf16[2048,256]{1,0:T(8,128)(2,1)S(1)} %collective-permute-done.32.refs_3_.refs_4_, bf16[2048,256]{1,0:T(8,128)(2,1)} %collective-permute-done.35.refs_7_, ...), kind=kLoop, calls=%fused_computation.2 | loop fusion | flops 3145728 | bytes 8388610 | tf_op jit(solution)/shard_map/jit(_where)/select_n | solution.py:364
  243.0 3.4 %copy-done.9 = bf16[2048,2048]{1,0:T(8,128)(2,1)S(1)} copy-done((bf16[2048,2048]{1,0:T(8,128)(2,1)S(1)}, bf16[2048,2048]{1,0:T(8,128)(2,1)}, u32[]{:S(2)}) %copy-start.9) | copy-done | bytes 8388632
  246.4 8.8 %shard_map.36 = (f32[2048,4096]{1,0:T(8,128)}, f32[8,128]{1,0:T(8,128)}) custom-call(s32[2]{0:T(128)S(1)} %get-tuple-element.321.blocks_ref, s32[1]{0:T(128)} %bitcast.3.place_ref, s32[2]{0:T(128)S(1)} %get-tuple-element.322.picks_ref, bf16[2048,2048]{1,0:T(8,128)(2,1)S(1)} %copy-done.9, ...), custom_call_target="tpu_custom_call", output_to_operand_aliasing={{0}: (12, {})} | custom-call | flops 4294967296 | bytes 14680064 | tf_op jit(solution)/shard_map/pallas_call | solution.py:188
  255.2 11.2 %shard_map.37 = (f32[2048,4096]{1,0:T(8,128)}, f32[8,128]{1,0:T(8,128)}) custom-call(s32[3]{0:T(128)S(1)} %pad_add_fusion.4.blocks_ref, s32[1]{0:T(128)} %bitcast.3.place_ref, s32[3]{0:T(128)S(1)} %broadcast_1_picks_ref.2.picks_ref, bf16[2048,2048]{1,0:T(8,128)(2,1)S(1)} %copy-done.9, ...), custom_call_target="tpu_custom_call", output_to_operand_aliasing={{0}: (7, {})} | custom-call | flops 6442450944 | bytes 17825792 | tf_op jit(solution)/shard_map/pallas_call | solution.py:188
  (158 shorter events, 110.9 us)
Async XLA Ops:
  2.7 20.0 %collective-permute-start = (bf16[2048,256]{1,0:T(8,128)(2,1)S(1)}, bf16[2048,256]{1,0:T(8,128)(2,1)S(1)}, u32[]{:S(2)}, u32[]{:S(2)}) collective-permute-start(bf16[2048,256]{1,0:T(8,128)(2,1)S(1)} %get-tuple-element.218.refs_0_), channel_id=1, source_target_pairs={{1,3},{3,1},{5,7},{7,5},{9,11},{11,9},{13,15},{15,13},{17,19},{19,... | collective-permute-start | bytes 3145736 | tf_op jit(solution)/shard_map/ppermute | solution.py:252
  42.3 18.2 %collective-permute-start.6 = (bf16[2048,256]{1,0:T(8,128)(2,1)}, bf16[2048,256]{1,0:T(8,128)(2,1)}, u32[]{:S(2)}, u32[]{:S(2)}) collective-permute-start(bf16[2048,256]{1,0:T(8,128)(2,1)} %collective-permute-done.2.refs_1_), channel_id=1, source_target_pairs={{8,0},{9,1},{10,2},{11,3},{12,4},{13,5},{14,6},{15,7},{16,24},{17,... | collective-permute-start | bytes 3145736 | tf_op jit(solution)/shard_map/ppermute | solution.py:252
  69.4 18.3 %collective-permute-start.12 = (bf16[2048,256]{1,0:T(8,128)(2,1)S(1)}, bf16[2048,256]{1,0:T(8,128)(2,1)}, u32[]{:S(2)}, u32[]{:S(2)}) collective-permute-start(bf16[2048,256]{1,0:T(8,128)(2,1)S(1)} %get-tuple-element.264.refs_1_.refs_0_), channel_id=1, source_target_pairs={{8,16},{9,17},{10,18},{11,19},{12,20},{13,21},{14,22},{15,23},{16,... | collective-permute-start | bytes 3145736 | tf_op jit(solution)/shard_map/ppermute | solution.py:252
  92.5 18.6 %collective-permute-start.16 = (bf16[2048,256]{1,0:T(8,128)(2,1)S(1)}, bf16[2048,256]{1,0:T(8,128)(2,1)S(1)}, u32[]{:S(2)}, u32[]{:S(2)}) collective-permute-start(bf16[2048,256]{1,0:T(8,128)(2,1)S(1)} %get-tuple-element.264.refs_1_.refs_0_), channel_id=1, source_target_pairs={{0,8},{1,9},{2,10},{3,11},{4,12},{5,13},{6,14},{7,15},{8,0},{9,1},... | collective-permute-start | bytes 3145736 | tf_op jit(solution)/shard_map/ppermute | solution.py:252
  97.5 19.0 %collective-permute-start.17 = (bf16[2048,256]{1,0:T(8,128)(2,1)}, bf16[2048,256]{1,0:T(8,128)(2,1)}, u32[]{:S(2)}, u32[]{:S(2)}) collective-permute-start(bf16[2048,256]{1,0:T(8,128)(2,1)} %get-tuple-element.308), channel_id=1, source_target_pairs={{0,4},{1,5},{2,6},{3,7},{4,0},{5,1},{6,2},{7,3},{8,12},{9,13},{10,... | collective-permute-start | bytes 3145736 | tf_op jit(solution)/shard_map/ppermute | solution.py:252
  98.9 18.4 %collective-permute-start.18 = (bf16[2048,256]{1,0:T(8,128)(2,1)}, bf16[2048,256]{1,0:T(8,128)(2,1)S(1)}, u32[]{:S(2)}, u32[]{:S(2)}) collective-permute-start(bf16[2048,256]{1,0:T(8,128)(2,1)} %get-tuple-element.304), channel_id=1, source_target_pairs={{0,2},{1,3},{2,0},{3,1},{4,6},{5,7},{6,4},{7,5},{8,10},{9,11},{10,... | collective-permute-start | bytes 3145736 | tf_op jit(solution)/shard_map/ppermute | solution.py:252
  98.9 18.4 %collective-permute-start.19 = (bf16[2048,256]{1,0:T(8,128)(2,1)}, bf16[2048,256]{1,0:T(8,128)(2,1)}, u32[]{:S(2)}, u32[]{:S(2)}) collective-permute-start(bf16[2048,256]{1,0:T(8,128)(2,1)} %collective-permute-done.9.refs_1_.refs_0_), channel_id=1, source_target_pairs={{0,1},{1,0},{2,3},{3,2},{4,5},{5,4},{6,7},{7,6},{8,9},{9,8},{10,11... | collective-permute-start | bytes 3145736 | tf_op jit(solution)/shard_map/ppermute | solution.py:252
  98.9 18.4 %collective-permute-start.20 = (bf16[2048,256]{1,0:T(8,128)(2,1)}, bf16[2048,256]{1,0:T(8,128)(2,1)}, u32[]{:S(2)}, u32[]{:S(2)}) collective-permute-start(bf16[2048,256]{1,0:T(8,128)(2,1)} %get-tuple-element.303), channel_id=1, source_target_pairs={{0,1},{1,0},{2,3},{3,2},{4,5},{5,4},{6,7},{7,6},{8,9},{9,8},{10,11... | collective-permute-start | bytes 3145736 | tf_op jit(solution)/shard_map/ppermute | solution.py:252
  117.3 21.8 %collective-permute-start.21 = (bf16[2048,256]{1,0:T(8,128)(2,1)}, bf16[2048,256]{1,0:T(8,128)(2,1)S(1)}, u32[]{:S(2)}, u32[]{:S(2)}) collective-permute-start(bf16[2048,256]{1,0:T(8,128)(2,1)} %collective-permute-done.12.refs_1_), channel_id=1, source_target_pairs={{8,0},{9,1},{10,2},{11,3},{12,4},{13,5},{14,6},{15,7},{16,24},{17,... | collective-permute-start | bytes 3145736 | tf_op jit(solution)/shard_map/ppermute | solution.py:252
  121.3 22.0 %collective-permute-start.22 = (bf16[2048,256]{1,0:T(8,128)(2,1)S(1)}, bf16[2048,256]{1,0:T(8,128)(2,1)}, u32[]{:S(2)}, u32[]{:S(2)}) collective-permute-start(bf16[2048,256]{1,0:T(8,128)(2,1)S(1)} %collective-permute-done.16.refs_3_), channel_id=1, source_target_pairs={{8,16},{9,17},{10,18},{11,19},{12,20},{13,21},{14,22},{15,23},{16,... | collective-permute-start | bytes 3145736 | tf_op jit(solution)/shard_map/ppermute | solution.py:252
  125.0 21.5 %collective-permute-start.23 = (bf16[2048,256]{1,0:T(8,128)(2,1)S(1)}, bf16[2048,256]{1,0:T(8,128)(2,1)S(1)}, u32[]{:S(2)}, u32[]{:S(2)}) collective-permute-start(bf16[2048,256]{1,0:T(8,128)(2,1)S(1)} %get-tuple-element.316), channel_id=1, source_target_pairs={{0,4},{1,5},{2,6},{3,7},{4,0},{5,1},{6,2},{7,3},{8,12},{9,13},{10,... | collective-permute-start | bytes 3145736 | tf_op jit(solution)/shard_map/ppermute | solution.py:252
  126.1 22.1 %collective-permute-start.24 = (bf16[2048,256]{1,0:T(8,128)(2,1)}, bf16[2048,256]{1,0:T(8,128)(2,1)S(1)}, u32[]{:S(2)}, u32[]{:S(2)}) collective-permute-start(bf16[2048,256]{1,0:T(8,128)(2,1)} %collective-permute-done.17.refs_6_), channel_id=1, source_target_pairs={{0,2},{1,3},{2,0},{3,1},{4,6},{5,7},{6,4},{7,5},{8,10},{9,11},{10,... | collective-permute-start | bytes 3145736 | tf_op jit(solution)/shard_map/ppermute | solution.py:252
  127.9 20.3 %collective-permute-start.25 = (bf16[2048,256]{1,0:T(8,128)(2,1)S(1)}, bf16[2048,256]{1,0:T(8,128)(2,1)S(1)}, u32[]{:S(2)}, u32[]{:S(2)}) collective-permute-start(bf16[2048,256]{1,0:T(8,128)(2,1)S(1)} %get-tuple-element.315), channel_id=1, source_target_pairs={{0,1},{1,0},{2,3},{3,2},{4,5},{5,4},{6,7},{7,6},{8,9},{9,8},{10,11... | collective-permute-start | bytes 3145736 | tf_op jit(solution)/shard_map/ppermute | solution.py:252
  148.2 31.2 %collective-permute-start.26 = (bf16[2048,256]{1,0:T(8,128)(2,1)}, bf16[2048,256]{1,0:T(8,128)(2,1)}, u32[]{:S(2)}, u32[]{:S(2)}) collective-permute-start(bf16[2048,256]{1,0:T(8,128)(2,1)} %collective-permute-done.22.refs_4_), channel_id=1, source_target_pairs={{8,0},{9,1},{10,2},{11,3},{12,4},{13,5},{14,6},{15,7},{16,24},{17,... | collective-permute-start | bytes 3145736 | tf_op jit(solution)/shard_map/ppermute | solution.py:252
  153.3 26.1 %collective-permute-start.27 = (bf16[2048,256]{1,0:T(8,128)(2,1)}, bf16[2048,256]{1,0:T(8,128)(2,1)}, u32[]{:S(2)}, u32[]{:S(2)}) collective-permute-start(bf16[2048,256]{1,0:T(8,128)(2,1)} %get-tuple-element.298), channel_id=1, source_target_pairs={{0,4},{1,5},{2,6},{3,7},{4,0},{5,1},{6,2},{7,3},{8,12},{9,13},{10,... | collective-permute-start | bytes 3145736 | tf_op jit(solution)/shard_map/ppermute | solution.py:252
  153.6 25.8 %collective-permute-start.28 = (bf16[2048,256]{1,0:T(8,128)(2,1)}, bf16[2048,256]{1,0:T(8,128)(2,1)S(1)}, u32[]{:S(2)}, u32[]{:S(2)}) collective-permute-start(bf16[2048,256]{1,0:T(8,128)(2,1)} %get-tuple-element.297), channel_id=1, source_target_pairs={{0,2},{1,3},{2,0},{3,1},{4,6},{5,7},{6,4},{7,5},{8,10},{9,11},{10,... | collective-permute-start | bytes 3145736 | tf_op jit(solution)/shard_map/ppermute | solution.py:252
  157.7 21.7 %collective-permute-start.29 = (bf16[2048,256]{1,0:T(8,128)(2,1)}, bf16[2048,256]{1,0:T(8,128)(2,1)}, u32[]{:S(2)}, u32[]{:S(2)}) collective-permute-start(bf16[2048,256]{1,0:T(8,128)(2,1)} %get-tuple-element.314), channel_id=1, source_target_pairs={{0,1},{1,0},{2,3},{3,2},{4,5},{5,4},{6,7},{7,6},{8,9},{9,8},{10,11... | collective-permute-start | bytes 3145736 | tf_op jit(solution)/shard_map/ppermute | solution.py:252
  157.7 21.7 %collective-permute-start.30 = (bf16[2048,256]{1,0:T(8,128)(2,1)}, bf16[2048,256]{1,0:T(8,128)(2,1)}, u32[]{:S(2)}, u32[]{:S(2)}) collective-permute-start(bf16[2048,256]{1,0:T(8,128)(2,1)} %get-tuple-element.313), channel_id=1, source_target_pairs={{0,1},{1,0},{2,3},{3,2},{4,5},{5,4},{6,7},{7,6},{8,9},{9,8},{10,11... | collective-permute-start | bytes 3145736 | tf_op jit(solution)/shard_map/ppermute | solution.py:252
  183.6 25.3 %collective-permute-start.31 = (bf16[2048,256]{1,0:T(8,128)(2,1)}, bf16[2048,256]{1,0:T(8,128)(2,1)}, u32[]{:S(2)}, u32[]{:S(2)}) collective-permute-start(bf16[2048,256]{1,0:T(8,128)(2,1)} %get-tuple-element.307), channel_id=1, source_target_pairs={{0,4},{1,5},{2,6},{3,7},{4,0},{5,1},{6,2},{7,3},{8,12},{9,13},{10,... | collective-permute-start | bytes 3145736 | tf_op jit(solution)/shard_map/ppermute | solution.py:252
  185.0 25.0 %collective-permute-start.32 = (bf16[2048,256]{1,0:T(8,128)(2,1)}, bf16[2048,256]{1,0:T(8,128)(2,1)S(1)}, u32[]{:S(2)}, u32[]{:S(2)}) collective-permute-start(bf16[2048,256]{1,0:T(8,128)(2,1)} %get-tuple-element.302), channel_id=1, source_target_pairs={{0,2},{1,3},{2,0},{3,1},{4,6},{5,7},{6,4},{7,5},{8,10},{9,11},{10,... | collective-permute-start | bytes 3145736 | tf_op jit(solution)/shard_map/ppermute | solution.py:252
  185.0 25.0 %collective-permute-start.33 = (bf16[2048,256]{1,0:T(8,128)(2,1)}, bf16[2048,256]{1,0:T(8,128)(2,1)}, u32[]{:S(2)}, u32[]{:S(2)}) collective-permute-start(bf16[2048,256]{1,0:T(8,128)(2,1)} %get-tuple-element.301), channel_id=1, source_target_pairs={{0,1},{1,0},{2,3},{3,2},{4,5},{5,4},{6,7},{7,6},{8,9},{9,8},{10,11... | collective-permute-start | bytes 3145736 | tf_op jit(solution)/shard_map/ppermute | solution.py:252
  212.8 24.3 %collective-permute-start.34 = (bf16[2048,256]{1,0:T(8,128)(2,1)}, bf16[2048,256]{1,0:T(8,128)(2,1)}, u32[]{:S(2)}, u32[]{:S(2)}) collective-permute-start(bf16[2048,256]{1,0:T(8,128)(2,1)} %get-tuple-element.312), channel_id=1, source_target_pairs={{0,4},{1,5},{2,6},{3,7},{4,0},{5,1},{6,2},{7,3},{8,12},{9,13},{10,... | collective-permute-start | bytes 3145736 | tf_op jit(solution)/shard_map/ppermute | solution.py:252
  213.2 24.1 %collective-permute-start.35 = (bf16[2048,256]{1,0:T(8,128)(2,1)}, bf16[2048,256]{1,0:T(8,128)(2,1)}, u32[]{:S(2)}, u32[]{:S(2)}) collective-permute-start(bf16[2048,256]{1,0:T(8,128)(2,1)} %collective-permute-done.31.refs_5_), channel_id=1, source_target_pairs={{0,2},{1,3},{2,0},{3,1},{4,6},{5,7},{6,4},{7,5},{8,10},{9,11},{10,... | collective-permute-start | bytes 3145736 | tf_op jit(solution)/shard_map/ppermute | solution.py:252
  213.4 23.9 %collective-permute-start.36 = (bf16[2048,256]{1,0:T(8,128)(2,1)}, bf16[2048,256]{1,0:T(8,128)(2,1)}, u32[]{:S(2)}, u32[]{:S(2)}) collective-permute-start(bf16[2048,256]{1,0:T(8,128)(2,1)} %get-tuple-element.311), channel_id=1, source_target_pairs={{0,1},{1,0},{2,3},{3,2},{4,5},{5,4},{6,7},{7,6},{8,9},{9,8},{10,11... | collective-permute-start | bytes 3145736 | tf_op jit(solution)/shard_map/ppermute | solution.py:252
  (53 other events, 648.2 us)

commit v2 on v0

--- a/solution.py
+++ b/solution.py
@@ -72,10 +72,6 @@
 
 def to_outer(z, x, y, c):
     return (z ^ 1, x, y, c) if inner(z) else None
-
-
-def to_back(z, x, y, c):
-    return (z, x, y ^ 1, c) if apart(z, y) == 0 else None
 
 
 def to_far(q):
@@ -236,11 +232,15 @@
         def send(name, value, target):
             running.append((name, lax.ppermute(value, AXES, lay.moves(target))))
 
-        def settle(barrier=True):
-            got.update(running)
-            running.clear()
-            if barrier:
-                got.update(zip(got, lax.optimization_barrier(tuple(got.values()))))
+        def settle(*under_way):
+            got.update(r for r in running if r[0][:2] not in under_way)
+            running[:] = [r for r in running if r[0][:2] in under_way]
+            got.update(zip(got, lax.optimization_barrier(tuple(got.values()))))
+
+        def take(kind, h, s, many):
+            mine = [r for r in running if r[0][:3] == (kind, h, s) and (r[0][3] > 0) == many]
+            got.update(mine)
+            running[:] = [r for r in running if r[0] not in [n for n, _ in mine]]
 
 
         def pair(h):
@@ -258,6 +258,15 @@
         def row(h):
             for m in others:
                 send(("row", h, m), got["own", h], along_y(m))
+
+        def row_of(core, h):
+            for m in others:
+                who = lambda z, x, y, c, m=m: (z, x, y ^ m, c) if c == core else None
+                send(("row_of", h, m, core), got["own", h], who)
+
+        def join_rows(h):
+            for m in others:
+                got["row", h, m] = jnp.where(c == 0, got["row_of", h, m, 0], got["row_of", h, m, 1])
 
         def give(h):
             for m in others:
@@ -297,7 +306,7 @@
 
         def back(h):
             for s in shifts:
-                send(("back", h, s), got["give_x", h, s, 1], to_back)
+                send(("back", h, s), got["give_x", h, s, 1], along_y(1))
 
 
         def mate(kind, h):
@@ -366,10 +375,13 @@
             else:
                 got["tile"], got["mark", "tile"] = multiply(tile, got["rows"], chunks, blocks, narrow_at, shape, width)
 
+        row_of(1, 0)
+        settle()
+
         pair(0)
         cross("own", 0)
         own_x(0)
-        row(0)
+        row_of(0, 0)
         mate("own", 0)
         settle()
 
@@ -384,13 +396,14 @@
         cross("own", 1)
         near_x(0)
         give(0)
+        join_rows(0)
         mate("row", 0)
         lay_row(0, 0)
         settle()
 
-        pair(1)
         give_x(0)
         give_more(0)
+        pair(1)
         mate("row", 1)
         swap("", 0)
         lay_row(0, 1)
@@ -403,6 +416,7 @@
         swap("y", 0)
         for m in others:
             lay_row(m, 0)
+        for m in others:
             lay_row(m, 1)
         settle()
 
@@ -423,12 +437,12 @@
         more_x(1)
         back(1)
         swap("y", 1)
-        product(1, "")
+        take("swapped", 1, 0, True)
+        product(1, "", "y")
         settle()
 
         swap("x", 1)
         swap("xy", 1)
-        product(1, "y")
         product(1, "x", "xy", sides=(0,))
         settle()
 

time: 280 us -> 263 us (0.939)
  starting transfers between devices: 72.9 us -> 52 us
  waiting for transfers between devices: 80.3 us -> 90.4 us
  local copies, waits for them, and re-layouts: 24.6 us -> 21.2 us
    ppermute x38 -> x39, starting transfers between devices: 72.9 us -> 52 us  [send(): running.append((name, lax.ppermute(value, AXES, lay.moves(target))))]
    ppermute x38 -> x39, waiting for transfers between devices: 80.3 us -> 90.4 us  [send(): running.append((name, lax.ppermute(value, AXES, lay.moves(target))))]
    unnamed x50, local copies, waits for them, and re-layouts: 23.9 us -> 20.5 us
    pallas_call x6 -> x5, Pallas kernels: 56.9 us -> 54.3 us  [multiply(): pl.pallas_call(kernel, grid_spec=pltpu.PrefetchScalarGridSpec(num_scalar_...]
  transfers between devices with their start and end apart: 38 -> 39, of which waited for: 21 -> 21; matrix products, arithmetic and copies ran while one was open for 6% -> 5% of each run, Pallas kernels for 21% -> 21%
where the time goes in v2:
time: 263 us; the launch traced here: 262 us
  waiting for transfers between devices  90.4 us (34%)
  Pallas kernels  63.8 us (24%)
  starting transfers between devices  52 us (20%)
  other arithmetic  34.2 us (13%)
  local copies, waits for them, and re-layouts  21.2 us (8%)
    ppermute x39, waiting for transfers between devices, send(): running.append((name, lax.ppermute(value, AXES, lay.moves(target))))  90.4 us
    pallas_call x5, Pallas kernels, multiply(): pl.pallas_call(kernel, grid_spec=pltpu.PrefetchScalarGridSpec(num_scalar_...  54.3 us
    ppermute x39, starting transfers between devices, send(): running.append((name, lax.ppermute(value, AXES, lay.moves(target))))  52 us
    unnamed x50, local copies, waits for them, and re-layouts  20.5 us
    select_n x6, other arithmetic, swap(): send(('swapped', h, s, m), jnp.where(first_kept, two, one), to_mate)  18.3 us
    pallas_call x4, Pallas kernels, turn(): pl.pallas_call(kernel, grid=(depth // TURN,), in_specs=in_specs, out_spec...  9.44 us
    select_n x2, other arithmetic, give_more(): value = jnp.where(off == m, got['own_x', h, 1], second(h, off ^ m))  6.12 us
    select_n x2, other arithmetic, give(): value = jnp.where(off == m, got['pair', h], first(h, off ^ m))  6.07 us
  transfers between devices with their start and end apart: 39, of which 21 were waited for; matrix products, arithmetic and copies ran while one was open for 5% of the time, Pallas kernels for 21%

profile of v2, /device:TPU:17, one launch (start us, length us, event | category | flops | bytes accessed | tf_op | source)
XLA Modules:
  0.0 262.1 jit_solution(27098687877098013)
XLA Ops:
  5.9 16.9 %collective-permute-done = bf16[2048,256]{1,0:T(8,128)(2,1)S(1)} collective-permute-done((bf16[2048,256]{1,0:T(8,128)(2,1)S(1)}, bf16[2048,256]{1,0:T(8,128)(2,1)S(1)}, u32[]{:S(2)}, u32[]{:S(2)}) %collective-permute-start) | collective-permute-done | bytes 1048608 | tf_op jit(solution)/shard_map/ppermute | solution.py:233
  30.0 7.3 %collective-permute-done.1 = bf16[2048,256]{1,0:T(8,128)(2,1)} collective-permute-done((bf16[2048,256]{1,0:T(8,128)(2,1)S(1)}, bf16[2048,256]{1,0:T(8,128)(2,1)}, u32[]{:S(2)}, u32[]{:S(2)}) %collective-permute-start.1) | collective-permute-done | bytes 1048608 | tf_op jit(solution)/shard_map/ppermute | solution.py:233
  42.4 6.3 %collective-permute-start.6 = (bf16[2048,256]{1,0:T(8,128)(2,1)}, bf16[2048,256]{1,0:T(8,128)(2,1)}, u32[]{:S(2)}, u32[]{:S(2)}) collective-permute-start(bf16[2048,256]{1,0:T(8,128)(2,1)} %collective-permute-done.2), channel_id=1, source_target_pairs={{8,0},{9,1},{10,2},{11,3},{12,4},{13,5},{14,6},{15,7},{16,24},{17,... | collective-permute-start | bytes 3145736 | tf_op jit(solution)/shard_map/ppermute | solution.py:233
  54.2 6.4 %collective-permute-done.6 = bf16[2048,256]{1,0:T(8,128)(2,1)} collective-permute-done((bf16[2048,256]{1,0:T(8,128)(2,1)}, bf16[2048,256]{1,0:T(8,128)(2,1)}, u32[]{:S(2)}, u32[]{:S(2)}) %collective-permute-start.6) | collective-permute-done | bytes 1048608 | tf_op jit(solution)/shard_map/ppermute | solution.py:233
  60.6 5.5 %collective-permute-done.7 = bf16[2048,256]{1,0:T(8,128)(2,1)} collective-permute-done((bf16[2048,256]{1,0:T(8,128)(2,1)}, bf16[2048,256]{1,0:T(8,128)(2,1)}, u32[]{:S(2)}, u32[]{:S(2)}) %collective-permute-start.7) | collective-permute-done | bytes 1048608 | tf_op jit(solution)/shard_map/ppermute | solution.py:233
  69.3 3.4 %collective-permute-start.12 = (bf16[2048,256]{1,0:T(8,128)(2,1)S(1)}, bf16[2048,256]{1,0:T(8,128)(2,1)}, u32[]{:S(2)}, u32[]{:S(2)}) collective-permute-start(bf16[2048,256]{1,0:T(8,128)(2,1)S(1)} %get-tuple-element.218.refs_1_), channel_id=1, source_target_pairs={{8,16},{9,17},{10,18},{11,19},{12,20},{13,21},{14,22},{15,23},{16,... | collective-permute-start | bytes 3145736 | tf_op jit(solution)/shard_map/ppermute | solution.py:233
  82.5 5.1 %collective-permute-done.12 = bf16[2048,256]{1,0:T(8,128)(2,1)} collective-permute-done((bf16[2048,256]{1,0:T(8,128)(2,1)S(1)}, bf16[2048,256]{1,0:T(8,128)(2,1)}, u32[]{:S(2)}, u32[]{:S(2)}) %collective-permute-start.12) | collective-permute-done | bytes 1048608 | tf_op jit(solution)/shard_map/ppermute | solution.py:233
  87.5 4.8 %collective-permute-done.13 = bf16[2048,256]{1,0:T(8,128)(2,1)} collective-permute-done((bf16[2048,256]{1,0:T(8,128)(2,1)}, bf16[2048,256]{1,0:T(8,128)(2,1)}, u32[]{:S(2)}, u32[]{:S(2)}) %collective-permute-start.13) | collective-permute-done | bytes 1048608 | tf_op jit(solution)/shard_map/ppermute | solution.py:233
  103.4 10.8 %collective-permute-done.16 = bf16[2048,256]{1,0:T(8,128)(2,1)S(1)} collective-permute-done((bf16[2048,256]{1,0:T(8,128)(2,1)S(1)}, bf16[2048,256]{1,0:T(8,128)(2,1)S(1)}, u32[]{:S(2)}, u32[]{:S(2)}) %collective-permute-start.16) | collective-permute-done | bytes 1048608 | tf_op jit(solution)/shard_map/ppermute | solution.py:233
  117.3 3.5 %collective-permute-start.21 = (bf16[2048,256]{1,0:T(8,128)(2,1)}, bf16[2048,256]{1,0:T(8,128)(2,1)S(1)}, u32[]{:S(2)}, u32[]{:S(2)}) collective-permute-start(bf16[2048,256]{1,0:T(8,128)(2,1)} %collective-permute-done.12), channel_id=1, source_target_pairs={{8,0},{9,1},{10,2},{11,3},{12,4},{13,5},{14,6},{15,7},{16,24},{17,... | collective-permute-start | bytes 3145736 | tf_op jit(solution)/shard_map/ppermute | solution.py:233
  133.0 3.6 %collective-permute-done.21 = bf16[2048,256]{1,0:T(8,128)(2,1)S(1)} collective-permute-done((bf16[2048,256]{1,0:T(8,128)(2,1)}, bf16[2048,256]{1,0:T(8,128)(2,1)S(1)}, u32[]{:S(2)}, u32[]{:S(2)}) %collective-permute-start.21) | collective-permute-done | bytes 1048608 | tf_op jit(solution)/shard_map/ppermute | solution.py:233
  155.4 3.4 %copy-done.1 = bf16[2048,2048]{1,0:T(8,128)(2,1)S(1)} copy-done((bf16[2048,2048]{1,0:T(8,128)(2,1)S(1)}, bf16[2048,2048]{1,0:T(8,128)(2,1)}, u32[]{:S(2)}) %copy-start.1) | copy-done | bytes 8388632
  163.7 12.0 %shard_map.32 = (f32[2048,4096]{1,0:T(8,128)}, f32[8,128]{1,0:T(8,128)}) custom-call(s32[4]{0:T(128)S(1)} %pad_add_fusion.1.blocks_ref, s32[1]{0:T(128)} %bitcast.2.place_ref, bf16[2048,2048]{1,0:T(8,128)(2,1)S(1)} %copy-done.1, bf16[2048,256]{1,0:T(8,128)(2,1)S(1)} %copy-done.10, bf16[2048,256]{1,0:T(8,128)(2,1)S(1)} %copy-done.13, ...), custom_call_target="tpu_custom_call" | custom-call | flops 8589934592 | bytes 20971520 | tf_op jit(solution)/shard_map/pallas_call | solution.py:171
  182.5 3.4 %copy-done.2 = bf16[2048,2048]{1,0:T(8,128)(2,1)S(1)} copy-done((bf16[2048,2048]{1,0:T(8,128)(2,1)S(1)}, bf16[2048,2048]{1,0:T(8,128)(2,1)}, u32[]{:S(2)}) %copy-start.2) | copy-done | bytes 8388632
  185.9 13.6 %shard_map.33 = (f32[2048,4096]{1,0:T(8,128)}, f32[8,128]{1,0:T(8,128)}) custom-call(s32[4]{0:T(128)S(1)} %pad_add_fusion.2.blocks_ref, s32[1]{0:T(128)} %bitcast.2.place_ref, bf16[2048,2048]{1,0:T(8,128)(2,1)S(1)} %copy-done.2, bf16[2048,256]{1,0:T(8,128)(2,1)S(1)} %get-tuple-element.226.refs_0_, ...), custom_call_target="tpu_custom_call", output_to_operand_aliasing={{0}: (7, {})} | custom-call | flops 8589934592 | bytes 20971520 | tf_op jit(solution)/shard_map/pallas_call | solution.py:171
  199.4 7.7 %collective-permute-done.31 = bf16[2048,256]{1,0:T(8,128)(2,1)} collective-permute-done((bf16[2048,256]{1,0:T(8,128)(2,1)}, bf16[2048,256]{1,0:T(8,128)(2,1)}, u32[]{:S(2)}, u32[]{:S(2)}) %collective-permute-start.31) | collective-permute-done | bytes 1048608 | tf_op jit(solution)/shard_map/ppermute | solution.py:233
  207.1 3.6 %broadcast_select_fusion.4 = (bf16[2048,256]{1,0:T(8,128)(2,1)}, bf16[2048,256]{1,0:T(8,128)(2,1)S(1)}, bf16[2048,256]{1,0:T(8,128)(2,1)}) fusion(pred[]{:T(512)S(6)} %eq.64, bf16[2048,256]{1,0:T(8,128)(2,1)S(1)} %copy-done.7, bf16[2048,256]{1,0:T(8,128)(2,1)} %collective-permute-done.28, pred[]{:T(512)S(6)} %eq.59, ...), kind=kLoop, calls=%fused_computation.16 | loop fusion | flops 3670016 | bytes 9437188 | tf_op jit(solution)/shard_map/jit(_where)/select_n | solution.py:344
  214.0 3.4 %copy-done.3 = bf16[2048,2048]{1,0:T(8,128)(2,1)S(1)} copy-done((bf16[2048,2048]{1,0:T(8,128)(2,1)S(1)}, bf16[2048,2048]{1,0:T(8,128)(2,1)}, u32[]{:S(2)}) %copy-start.3) | copy-done | bytes 8388632
  217.4 13.2 %shard_map.34 = (f32[2048,4096]{1,0:T(8,128)}, f32[8,128]{1,0:T(8,128)}) custom-call(s32[4]{0:T(128)S(1)} %pad_add_fusion.3.blocks_ref, s32[1]{0:T(128)} %bitcast.2.place_ref, bf16[2048,2048]{1,0:T(8,128)(2,1)S(1)} %copy-done.3, bf16[2048,256]{1,0:T(8,128)(2,1)S(1)} %get-tuple-element.240.refs_0_, ...), custom_call_target="tpu_custom_call", output_to_operand_aliasing={{0}: (7, {})} | custom-call | flops 8589934592 | bytes 20971520 | tf_op jit(solution)/shard_map/pallas_call | solution.py:171
  230.6 6.1 %collective-permute-done.35 = bf16[2048,256]{1,0:T(8,128)(2,1)} collective-permute-done((bf16[2048,256]{1,0:T(8,128)(2,1)}, bf16[2048,256]{1,0:T(8,128)(2,1)}, u32[]{:S(2)}, u32[]{:S(2)}) %collective-permute-start.35) | collective-permute-done | bytes 1048608 | tf_op jit(solution)/shard_map/ppermute | solution.py:233
  237.8 3.9 %broadcast_select_fusion = (bf16[2048,256]{1,0:T(8,128)(2,1)}, bf16[2048,256]{1,0:T(8,128)(2,1)S(1)}, bf16[2048,256]{1,0:T(8,128)(2,1)S(1)}, bf16[2048,256]{1,0:T(8,128)(2,1)}) fusion(pred[]{:T(512)S(6)} %eq.64, bf16[2048,256]{1,0:T(8,128)(2,1)} %collective-permute-done.32, bf16[2048,256]{1,0:T(8,128)(2,1)} %collective-permute-done.31, pred[]{:T(512)S(6)} %eq.59, ...), kind=kLoop, calls=%fused_computation.12 | loop fusion | flops 4194304 | bytes 10485762 | tf_op jit(solution)/shard_map/jit(_where)/select_n | solution.py:344
  242.9 3.4 %copy-done.4 = bf16[2048,2048]{1,0:T(8,128)(2,1)S(1)} copy-done((bf16[2048,2048]{1,0:T(8,128)(2,1)S(1)}, bf16[2048,2048]{1,0:T(8,128)(2,1)}, u32[]{:S(2)}) %copy-start.4) | copy-done | bytes 8388632
  246.3 7.2 %shard_map.35 = (f32[2048,4096]{1,0:T(8,128)}, f32[8,128]{1,0:T(8,128)}) custom-call(s32[2]{0:T(128)S(1)} %pad_add_fusion.4.blocks_ref, s32[1]{0:T(128)} %bitcast.2.place_ref, bf16[2048,2048]{1,0:T(8,128)(2,1)S(1)} %copy-done.4, bf16[2048,256]{1,0:T(8,128)(2,1)S(1)} %get-tuple-element.291.refs_0_, ...), custom_call_target="tpu_custom_call", output_to_operand_aliasing={{0}: (5, {})} | custom-call | flops 4294967296 | bytes 14680064 | tf_op jit(solution)/shard_map/pallas_call | solution.py:171
  253.5 8.4 %shard_map.36 = (f32[2048,4096]{1,0:T(8,128)}, f32[8,128]{1,0:T(8,128)}) custom-call(s32[2]{0:T(128)S(1)} %pad_add_fusion.blocks_ref, s32[1]{0:T(128)} %bitcast.2.place_ref, bf16[2048,2048]{1,0:T(8,128)(2,1)S(1)} %copy-done.4, bf16[2048,256]{1,0:T(8,128)(2,1)S(1)} %collective-permute-done.37.refs_0_, ...), custom_call_target="tpu_custom_call", output_to_operand_aliasing={{0}: (5, {})} | custom-call | flops 4294967296 | bytes 14680064 | tf_op jit(solution)/shard_map/pallas_call | solution.py:171
  (131 shorter events, 99.2 us)
Async XLA Ops:
  2.7 20.0 %collective-permute-start = (bf16[2048,256]{1,0:T(8,128)(2,1)S(1)}, bf16[2048,256]{1,0:T(8,128)(2,1)S(1)}, u32[]{:S(2)}, u32[]{:S(2)}) collective-permute-start(bf16[2048,256]{1,0:T(8,128)(2,1)S(1)} %get-tuple-element.159.refs_0_), channel_id=1, source_target_pairs={{1,3},{3,1},{5,7},{7,5},{9,11},{11,9},{13,15},{15,13},{17,19},{19,... | collective-permute-start | bytes 3145736 | tf_op jit(solution)/shard_map/ppermute | solution.py:233
  25.0 15.6 %collective-permute-start.2 = (bf16[2048,256]{1,0:T(8,128)(2,1)S(1)}, bf16[2048,256]{1,0:T(8,128)(2,1)}, u32[]{:S(2)}, u32[]{:S(2)}) collective-permute-start(bf16[2048,256]{1,0:T(8,128)(2,1)S(1)} %get-tuple-element.159.refs_0_), channel_id=1, source_target_pairs={{8,16},{9,17},{10,18},{11,19},{12,20},{13,21},{14,22},{15,23},{16,... | collective-permute-start | bytes 3145736 | tf_op jit(solution)/shard_map/ppermute | solution.py:233
  42.4 18.2 %collective-permute-start.6 = (bf16[2048,256]{1,0:T(8,128)(2,1)}, bf16[2048,256]{1,0:T(8,128)(2,1)}, u32[]{:S(2)}, u32[]{:S(2)}) collective-permute-start(bf16[2048,256]{1,0:T(8,128)(2,1)} %collective-permute-done.2), channel_id=1, source_target_pairs={{8,0},{9,1},{10,2},{11,3},{12,4},{13,5},{14,6},{15,7},{16,24},{17,... | collective-permute-start | bytes 3145736 | tf_op jit(solution)/shard_map/ppermute | solution.py:233
  48.7 17.5 %collective-permute-start.7 = (bf16[2048,256]{1,0:T(8,128)(2,1)}, bf16[2048,256]{1,0:T(8,128)(2,1)}, u32[]{:S(2)}, u32[]{:S(2)}) collective-permute-start(bf16[2048,256]{1,0:T(8,128)(2,1)} %collective-permute-done.1), channel_id=1, source_target_pairs={{8,16},{9,17},{10,18},{11,19},{12,20},{13,21},{14,22},{15,23},{16,... | collective-permute-start | bytes 3145736 | tf_op jit(solution)/shard_map/ppermute | solution.py:233
  69.3 18.3 %collective-permute-start.12 = (bf16[2048,256]{1,0:T(8,128)(2,1)S(1)}, bf16[2048,256]{1,0:T(8,128)(2,1)}, u32[]{:S(2)}, u32[]{:S(2)}) collective-permute-start(bf16[2048,256]{1,0:T(8,128)(2,1)S(1)} %get-tuple-element.218.refs_1_), channel_id=1, source_target_pairs={{8,16},{9,17},{10,18},{11,19},{12,20},{13,21},{14,22},{15,23},{16,... | collective-permute-start | bytes 3145736 | tf_op jit(solution)/shard_map/ppermute | solution.py:233
  75.8 16.5 %collective-permute-start.13 = (bf16[2048,256]{1,0:T(8,128)(2,1)}, bf16[2048,256]{1,0:T(8,128)(2,1)}, u32[]{:S(2)}, u32[]{:S(2)}) collective-permute-start(bf16[2048,256]{1,0:T(8,128)(2,1)} %get-tuple-element.276), channel_id=1, source_target_pairs={{0,4},{1,5},{2,6},{3,7},{4,0},{5,1},{6,2},{7,3},{8,12},{9,13},{10,... | collective-permute-start | bytes 3145736 | tf_op jit(solution)/shard_map/ppermute | solution.py:233
  76.5 15.9 %collective-permute-start.14 = (bf16[2048,256]{1,0:T(8,128)(2,1)}, bf16[2048,256]{1,0:T(8,128)(2,1)}, u32[]{:S(2)}, u32[]{:S(2)}) collective-permute-start(bf16[2048,256]{1,0:T(8,128)(2,1)} %get-tuple-element.275), channel_id=1, source_target_pairs={{0,2},{1,3},{2,0},{3,1},{4,6},{5,7},{6,4},{7,5},{8,10},{9,11},{10,... | collective-permute-start | bytes 3145736 | tf_op jit(solution)/shard_map/ppermute | solution.py:233
  97.3 16.9 %collective-permute-start.16 = (bf16[2048,256]{1,0:T(8,128)(2,1)S(1)}, bf16[2048,256]{1,0:T(8,128)(2,1)S(1)}, u32[]{:S(2)}, u32[]{:S(2)}) collective-permute-start(bf16[2048,256]{1,0:T(8,128)(2,1)S(1)} %get-tuple-element.298), channel_id=1, source_target_pairs={{0,4},{1,5},{2,6},{3,7},{4,0},{5,1},{6,2},{7,3},{8,12},{9,13},{10,... | collective-permute-start | bytes 3145736 | tf_op jit(solution)/shard_map/ppermute | solution.py:233
  98.9 17.3 %collective-permute-start.17 = (bf16[2048,256]{1,0:T(8,128)(2,1)S(1)}, bf16[2048,256]{1,0:T(8,128)(2,1)S(1)}, u32[]{:S(2)}, u32[]{:S(2)}) collective-permute-start(bf16[2048,256]{1,0:T(8,128)(2,1)S(1)} %get-tuple-element.289), channel_id=1, source_target_pairs={{0,2},{1,3},{2,0},{3,1},{4,6},{5,7},{6,4},{7,5},{8,10},{9,11},{10,... | collective-permute-start | bytes 3145736 | tf_op jit(solution)/shard_map/ppermute | solution.py:233
  99.7 16.6 %collective-permute-start.18 = (bf16[2048,256]{1,0:T(8,128)(2,1)S(1)}, bf16[2048,256]{1,0:T(8,128)(2,1)S(1)}, u32[]{:S(2)}, u32[]{:S(2)}) collective-permute-start(bf16[2048,256]{1,0:T(8,128)(2,1)S(1)} %get-tuple-element.218.refs_1_), channel_id=1, source_target_pairs={{0,8},{1,9},{2,10},{3,11},{4,12},{5,13},{6,14},{7,15},{8,0},{9,1},... | collective-permute-start | bytes 3145736 | tf_op jit(solution)/shard_map/ppermute | solution.py:233
  99.7 16.6 %collective-permute-start.19 = (bf16[2048,256]{1,0:T(8,128)(2,1)S(1)}, bf16[2048,256]{1,0:T(8,128)(2,1)S(1)}, u32[]{:S(2)}, u32[]{:S(2)}) collective-permute-start(bf16[2048,256]{1,0:T(8,128)(2,1)S(1)} %copy-done.6), channel_id=1, source_target_pairs={{0,1},{1,0},{2,3},{3,2},{4,5},{5,4},{6,7},{7,6},{8,9},{9,8},{10,11... | collective-permute-start | bytes 3145736 | tf_op jit(solution)/shard_map/ppermute | solution.py:233
  99.7 16.6 %collective-permute-start.20 = (bf16[2048,256]{1,0:T(8,128)(2,1)S(1)}, bf16[2048,256]{1,0:T(8,128)(2,1)S(1)}, u32[]{:S(2)}, u32[]{:S(2)}) collective-permute-start(bf16[2048,256]{1,0:T(8,128)(2,1)S(1)} %get-tuple-element.266), channel_id=1, source_target_pairs={{0,1},{1,0},{2,3},{3,2},{4,5},{5,4},{6,7},{7,6},{8,9},{9,8},{10,11... | collective-permute-start | bytes 3145736 | tf_op jit(solution)/shard_map/ppermute | solution.py:233
  117.3 19.3 %collective-permute-start.21 = (bf16[2048,256]{1,0:T(8,128)(2,1)}, bf16[2048,256]{1,0:T(8,128)(2,1)S(1)}, u32[]{:S(2)}, u32[]{:S(2)}) collective-permute-start(bf16[2048,256]{1,0:T(8,128)(2,1)} %collective-permute-done.12), channel_id=1, source_target_pairs={{8,0},{9,1},{10,2},{11,3},{12,4},{13,5},{14,6},{15,7},{16,24},{17,... | collective-permute-start | bytes 3145736 | tf_op jit(solution)/shard_map/ppermute | solution.py:233
  120.8 17.4 %collective-permute-start.22 = (bf16[2048,256]{1,0:T(8,128)(2,1)S(1)}, bf16[2048,256]{1,0:T(8,128)(2,1)}, u32[]{:S(2)}, u32[]{:S(2)}) collective-permute-start(bf16[2048,256]{1,0:T(8,128)(2,1)S(1)} %collective-permute-done.18), channel_id=1, source_target_pairs={{8,16},{9,17},{10,18},{11,19},{12,20},{13,21},{14,22},{15,23},{16,... | collective-permute-start | bytes 3145736 | tf_op jit(solution)/shard_map/ppermute | solution.py:233
  142.0 33.7 %collective-permute-start.26 = (bf16[2048,256]{1,0:T(8,128)(2,1)}, bf16[2048,256]{1,0:T(8,128)(2,1)}, u32[]{:S(2)}, u32[]{:S(2)}) collective-permute-start(bf16[2048,256]{1,0:T(8,128)(2,1)} %collective-permute-done.22), channel_id=1, source_target_pairs={{8,0},{9,1},{10,2},{11,3},{12,4},{13,5},{14,6},{15,7},{16,24},{17,... | collective-permute-start | bytes 3145736 | tf_op jit(solution)/shard_map/ppermute | solution.py:233
  147.2 28.5 %collective-permute-start.27 = (bf16[2048,256]{1,0:T(8,128)(2,1)}, bf16[2048,256]{1,0:T(8,128)(2,1)}, u32[]{:S(2)}, u32[]{:S(2)}) collective-permute-start(bf16[2048,256]{1,0:T(8,128)(2,1)} %get-tuple-element.274), channel_id=1, source_target_pairs={{0,4},{1,5},{2,6},{3,7},{4,0},{5,1},{6,2},{7,3},{8,12},{9,13},{10,... | collective-permute-start | bytes 3145736 | tf_op jit(solution)/shard_map/ppermute | solution.py:233
  150.0 25.7 %collective-permute-start.28 = (bf16[2048,256]{1,0:T(8,128)(2,1)}, bf16[2048,256]{1,0:T(8,128)(2,1)}, u32[]{:S(2)}, u32[]{:S(2)}) collective-permute-start(bf16[2048,256]{1,0:T(8,128)(2,1)} %get-tuple-element.273), channel_id=1, source_target_pairs={{0,2},{1,3},{2,0},{3,1},{4,6},{5,7},{6,4},{7,5},{8,10},{9,11},{10,... | collective-permute-start | bytes 3145736 | tf_op jit(solution)/shard_map/ppermute | solution.py:233
  154.8 21.0 %collective-permute-start.29 = (bf16[2048,256]{1,0:T(8,128)(2,1)}, bf16[2048,256]{1,0:T(8,128)(2,1)}, u32[]{:S(2)}, u32[]{:S(2)}) collective-permute-start(bf16[2048,256]{1,0:T(8,128)(2,1)} %get-tuple-element.296), channel_id=1, source_target_pairs={{0,1},{1,0},{2,3},{3,2},{4,5},{5,4},{6,7},{7,6},{8,9},{9,8},{10,11... | collective-permute-start | bytes 3145736 | tf_op jit(solution)/shard_map/ppermute | solution.py:233
  154.8 20.9 %collective-permute-start.30 = (bf16[2048,256]{1,0:T(8,128)(2,1)}, bf16[2048,256]{1,0:T(8,128)(2,1)}, u32[]{:S(2)}, u32[]{:S(2)}) collective-permute-start(bf16[2048,256]{1,0:T(8,128)(2,1)} %get-tuple-element.271), channel_id=1, source_target_pairs={{0,1},{1,0},{2,3},{3,2},{4,5},{5,4},{6,7},{7,6},{8,9},{9,8},{10,11... | collective-permute-start | bytes 3145736 | tf_op jit(solution)/shard_map/ppermute | solution.py:233
  182.0 25.1 %collective-permute-start.31 = (bf16[2048,256]{1,0:T(8,128)(2,1)}, bf16[2048,256]{1,0:T(8,128)(2,1)}, u32[]{:S(2)}, u32[]{:S(2)}) collective-permute-start(bf16[2048,256]{1,0:T(8,128)(2,1)} %get-tuple-element.294), channel_id=1, source_target_pairs={{0,4},{1,5},{2,6},{3,7},{4,0},{5,1},{6,2},{7,3},{8,12},{9,13},{10,... | collective-permute-start | bytes 3145736 | tf_op jit(solution)/shard_map/ppermute | solution.py:233
  182.0 25.0 %collective-permute-start.32 = (bf16[2048,256]{1,0:T(8,128)(2,1)}, bf16[2048,256]{1,0:T(8,128)(2,1)}, u32[]{:S(2)}, u32[]{:S(2)}) collective-permute-start(bf16[2048,256]{1,0:T(8,128)(2,1)} %get-tuple-element.287), channel_id=1, source_target_pairs={{0,2},{1,3},{2,0},{3,1},{4,6},{5,7},{6,4},{7,5},{8,10},{9,11},{10,... | collective-permute-start | bytes 3145736 | tf_op jit(solution)/shard_map/ppermute | solution.py:233
  182.0 25.0 %collective-permute-start.33 = (bf16[2048,256]{1,0:T(8,128)(2,1)}, bf16[2048,256]{1,0:T(8,128)(2,1)}, u32[]{:S(2)}, u32[]{:S(2)}) collective-permute-start(bf16[2048,256]{1,0:T(8,128)(2,1)} %get-tuple-element.263), channel_id=1, source_target_pairs={{0,1},{1,0},{2,3},{3,2},{4,5},{5,4},{6,7},{7,6},{8,9},{9,8},{10,11... | collective-permute-start | bytes 3145736 | tf_op jit(solution)/shard_map/ppermute | solution.py:233
  211.5 25.1 %collective-permute-start.35 = (bf16[2048,256]{1,0:T(8,128)(2,1)}, bf16[2048,256]{1,0:T(8,128)(2,1)}, u32[]{:S(2)}, u32[]{:S(2)}) collective-permute-start(bf16[2048,256]{1,0:T(8,128)(2,1)} %get-tuple-element.293), channel_id=1, source_target_pairs={{0,4},{1,5},{2,6},{3,7},{4,0},{5,1},{6,2},{7,3},{8,12},{9,13},{10,... | collective-permute-start | bytes 3145736 | tf_op jit(solution)/shard_map/ppermute | solution.py:233
  213.0 24.8 %collective-permute-start.36 = (bf16[2048,256]{1,0:T(8,128)(2,1)}, bf16[2048,256]{1,0:T(8,128)(2,1)}, u32[]{:S(2)}, u32[]{:S(2)}) collective-permute-start(bf16[2048,256]{1,0:T(8,128)(2,1)} %collective-permute-done.31), channel_id=1, source_target_pairs={{0,2},{1,3},{2,0},{3,1},{4,6},{5,7},{6,4},{7,5},{8,10},{9,11},{10,... | collective-permute-start | bytes 3145736 | tf_op jit(solution)/shard_map/ppermute | solution.py:233
  (40 other events, 439.0 us)

commit v3 on v2

--- a/solution.py
+++ b/solution.py
@@ -10,7 +10,7 @@
 LANES = 128
 PARTS = 2
 TURN = 512
-VMEM_MIB = 24
+VMEM_MIB = 36
 
 
 class Layout:

time: 263 us -> 262 us (level)
  no operation moved by 1% of the time
where the time goes in v3:
time: 262 us; the launch traced here: 261 us
  waiting for transfers between devices  89.7 us (34%)
  Pallas kernels  63.7 us (24%)
  starting transfers between devices  53.3 us (20%)
  other arithmetic  33.8 us (13%)
  local copies, waits for them, and re-layouts  20.2 us (8%)
    ppermute x39, waiting for transfers between devices, send(): running.append((name, lax.ppermute(value, AXES, lay.moves(target))))  89.7 us
    pallas_call x5, Pallas kernels, multiply(): pl.pallas_call(kernel, grid_spec=pltpu.PrefetchScalarGridSpec(num_scalar_...  54.3 us
    ppermute x39, starting transfers between devices, send(): running.append((name, lax.ppermute(value, AXES, lay.moves(target))))  53.3 us
    unnamed x50, local copies, waits for them, and re-layouts  19.5 us
    select_n x6, other arithmetic, swap(): send(('swapped', h, s, m), jnp.where(first_kept, two, one), to_mate)  18.1 us
    pallas_call x4, Pallas kernels, turn(): pl.pallas_call(kernel, grid=(depth // TURN,), in_specs=in_specs, out_spec...  9.44 us
    select_n x2, other arithmetic, give_more(): value = jnp.where(off == m, got['own_x', h, 1], second(h, off ^ m))  6.05 us
    select_n x2, other arithmetic, give(): value = jnp.where(off == m, got['pair', h], first(h, off ^ m))  5.98 us
  transfers between devices with their start and end apart: 39, of which 21 were waited for; matrix products, arithmetic and copies ran while one was open for 5% of the time, Pallas kernels for 21%

profile of v3, /device:TPU:17, one launch (start us, length us, event | category | flops | bytes accessed | tf_op | source)
XLA Modules:
  0.0 261.2 jit_solution(3149016509932622633)
XLA Ops:
  5.9 16.9 %collective-permute-done = bf16[2048,256]{1,0:T(8,128)(2,1)S(1)} collective-permute-done((bf16[2048,256]{1,0:T(8,128)(2,1)S(1)}, bf16[2048,256]{1,0:T(8,128)(2,1)S(1)}, u32[]{:S(2)}, u32[]{:S(2)}) %collective-permute-start) | collective-permute-done | bytes 1048608 | tf_op jit(solution)/shard_map/ppermute | solution.py:233
  30.0 7.3 %collective-permute-done.1 = bf16[2048,256]{1,0:T(8,128)(2,1)} collective-permute-done((bf16[2048,256]{1,0:T(8,128)(2,1)S(1)}, bf16[2048,256]{1,0:T(8,128)(2,1)}, u32[]{:S(2)}, u32[]{:S(2)}) %collective-permute-start.1) | collective-permute-done | bytes 1048608 | tf_op jit(solution)/shard_map/ppermute | solution.py:233
  42.4 6.3 %collective-permute-start.6 = (bf16[2048,256]{1,0:T(8,128)(2,1)}, bf16[2048,256]{1,0:T(8,128)(2,1)}, u32[]{:S(2)}, u32[]{:S(2)}) collective-permute-start(bf16[2048,256]{1,0:T(8,128)(2,1)} %collective-permute-done.2), channel_id=1, source_target_pairs={{8,0},{9,1},{10,2},{11,3},{12,4},{13,5},{14,6},{15,7},{16,24},{17,... | collective-permute-start | bytes 3145736 | tf_op jit(solution)/shard_map/ppermute | solution.py:233
  54.2 6.4 %collective-permute-done.6 = bf16[2048,256]{1,0:T(8,128)(2,1)} collective-permute-done((bf16[2048,256]{1,0:T(8,128)(2,1)}, bf16[2048,256]{1,0:T(8,128)(2,1)}, u32[]{:S(2)}, u32[]{:S(2)}) %collective-permute-start.6) | collective-permute-done | bytes 1048608 | tf_op jit(solution)/shard_map/ppermute | solution.py:233
  60.6 5.5 %collective-permute-done.7 = bf16[2048,256]{1,0:T(8,128)(2,1)} collective-permute-done((bf16[2048,256]{1,0:T(8,128)(2,1)}, bf16[2048,256]{1,0:T(8,128)(2,1)}, u32[]{:S(2)}, u32[]{:S(2)}) %collective-permute-start.7) | collective-permute-done | bytes 1048608 | tf_op jit(solution)/shard_map/ppermute | solution.py:233
  69.3 3.4 %collective-permute-start.12 = (bf16[2048,256]{1,0:T(8,128)(2,1)S(1)}, bf16[2048,256]{1,0:T(8,128)(2,1)}, u32[]{:S(2)}, u32[]{:S(2)}) collective-permute-start(bf16[2048,256]{1,0:T(8,128)(2,1)S(1)} %get-tuple-element.218.refs_1_), channel_id=1, source_target_pairs={{8,16},{9,17},{10,18},{11,19},{12,20},{13,21},{14,22},{15,23},{16,... | collective-permute-start | bytes 3145736 | tf_op jit(solution)/shard_map/ppermute | solution.py:233
  82.5 5.1 %collective-permute-done.12 = bf16[2048,256]{1,0:T(8,128)(2,1)} collective-permute-done((bf16[2048,256]{1,0:T(8,128)(2,1)S(1)}, bf16[2048,256]{1,0:T(8,128)(2,1)}, u32[]{:S(2)}, u32[]{:S(2)}) %collective-permute-start.12) | collective-permute-done | bytes 1048608 | tf_op jit(solution)/shard_map/ppermute | solution.py:233
  87.5 4.8 %collective-permute-done.13 = bf16[2048,256]{1,0:T(8,128)(2,1)} collective-permute-done((bf16[2048,256]{1,0:T(8,128)(2,1)}, bf16[2048,256]{1,0:T(8,128)(2,1)}, u32[]{:S(2)}, u32[]{:S(2)}) %collective-permute-start.13) | collective-permute-done | bytes 1048608 | tf_op jit(solution)/shard_map/ppermute | solution.py:233
  103.4 10.8 %collective-permute-done.16 = bf16[2048,256]{1,0:T(8,128)(2,1)S(1)} collective-permute-done((bf16[2048,256]{1,0:T(8,128)(2,1)S(1)}, bf16[2048,256]{1,0:T(8,128)(2,1)S(1)}, u32[]{:S(2)}, u32[]{:S(2)}) %collective-permute-start.16) | collective-permute-done | bytes 1048608 | tf_op jit(solution)/shard_map/ppermute | solution.py:233
  116.6 4.2 %collective-permute-start.21 = (bf16[2048,256]{1,0:T(8,128)(2,1)}, bf16[2048,256]{1,0:T(8,128)(2,1)S(1)}, u32[]{:S(2)}, u32[]{:S(2)}) collective-permute-start(bf16[2048,256]{1,0:T(8,128)(2,1)} %collective-permute-done.12), channel_id=1, source_target_pairs={{8,0},{9,1},{10,2},{11,3},{12,4},{13,5},{14,6},{15,7},{16,24},{17,... | collective-permute-start | bytes 3145736 | tf_op jit(solution)/shard_map/ppermute | solution.py:233
  133.0 3.5 %collective-permute-done.21 = bf16[2048,256]{1,0:T(8,128)(2,1)S(1)} collective-permute-done((bf16[2048,256]{1,0:T(8,128)(2,1)}, bf16[2048,256]{1,0:T(8,128)(2,1)S(1)}, u32[]{:S(2)}, u32[]{:S(2)}) %collective-permute-start.21) | collective-permute-done | bytes 1048608 | tf_op jit(solution)/shard_map/ppermute | solution.py:233
  154.8 3.4 %copy-done.1 = bf16[2048,2048]{1,0:T(8,128)(2,1)S(1)} copy-done((bf16[2048,2048]{1,0:T(8,128)(2,1)S(1)}, bf16[2048,2048]{1,0:T(8,128)(2,1)}, u32[]{:S(2)}) %copy-start.1) | copy-done | bytes 8388632
  163.1 11.9 %shard_map.32 = (f32[2048,4096]{1,0:T(8,128)}, f32[8,128]{1,0:T(8,128)}) custom-call(s32[4]{0:T(128)S(1)} %pad_add_fusion.1.blocks_ref, s32[1]{0:T(128)} %bitcast.2.place_ref, bf16[2048,2048]{1,0:T(8,128)(2,1)S(1)} %copy-done.1, bf16[2048,256]{1,0:T(8,128)(2,1)S(1)} %copy-done.10, bf16[2048,256]{1,0:T(8,128)(2,1)S(1)} %copy-done.13, ...), custom_call_target="tpu_custom_call" | custom-call | flops 8589934592 | bytes 20971520 | tf_op jit(solution)/shard_map/pallas_call | solution.py:171
  181.7 3.4 %copy-done.2 = bf16[2048,2048]{1,0:T(8,128)(2,1)S(1)} copy-done((bf16[2048,2048]{1,0:T(8,128)(2,1)S(1)}, bf16[2048,2048]{1,0:T(8,128)(2,1)}, u32[]{:S(2)}) %copy-start.2) | copy-done | bytes 8388632
  185.0 13.5 %shard_map.33 = (f32[2048,4096]{1,0:T(8,128)}, f32[8,128]{1,0:T(8,128)}) custom-call(s32[4]{0:T(128)S(1)} %pad_add_fusion.2.blocks_ref, s32[1]{0:T(128)} %bitcast.2.place_ref, bf16[2048,2048]{1,0:T(8,128)(2,1)S(1)} %copy-done.2, bf16[2048,256]{1,0:T(8,128)(2,1)S(1)} %get-tuple-element.226.refs_0_, ...), custom_call_target="tpu_custom_call", output_to_operand_aliasing={{0}: (7, {})} | custom-call | flops 8589934592 | bytes 20971520 | tf_op jit(solution)/shard_map/pallas_call | solution.py:171
  198.6 7.7 %collective-permute-done.31 = bf16[2048,256]{1,0:T(8,128)(2,1)} collective-permute-done((bf16[2048,256]{1,0:T(8,128)(2,1)}, bf16[2048,256]{1,0:T(8,128)(2,1)}, u32[]{:S(2)}, u32[]{:S(2)}) %collective-permute-start.31) | collective-permute-done | bytes 1048608 | tf_op jit(solution)/shard_map/ppermute | solution.py:233
  206.3 3.5 %broadcast_select_fusion.4 = (bf16[2048,256]{1,0:T(8,128)(2,1)}, bf16[2048,256]{1,0:T(8,128)(2,1)S(1)}, bf16[2048,256]{1,0:T(8,128)(2,1)}) fusion(pred[]{:T(512)S(6)} %eq.64, bf16[2048,256]{1,0:T(8,128)(2,1)S(1)} %copy-done.7, bf16[2048,256]{1,0:T(8,128)(2,1)} %collective-permute-done.28, pred[]{:T(512)S(6)} %eq.59, ...), kind=kLoop, calls=%fused_computation.16 | loop fusion | flops 3670016 | bytes 9437188 | tf_op jit(solution)/shard_map/jit(_where)/select_n | solution.py:344
  213.1 3.4 %copy-done.3 = bf16[2048,2048]{1,0:T(8,128)(2,1)S(1)} copy-done((bf16[2048,2048]{1,0:T(8,128)(2,1)S(1)}, bf16[2048,2048]{1,0:T(8,128)(2,1)}, u32[]{:S(2)}) %copy-start.3) | copy-done | bytes 8388632
  216.5 13.2 %shard_map.34 = (f32[2048,4096]{1,0:T(8,128)}, f32[8,128]{1,0:T(8,128)}) custom-call(s32[4]{0:T(128)S(1)} %pad_add_fusion.3.blocks_ref, s32[1]{0:T(128)} %bitcast.2.place_ref, bf16[2048,2048]{1,0:T(8,128)(2,1)S(1)} %copy-done.3, bf16[2048,256]{1,0:T(8,128)(2,1)S(1)} %get-tuple-element.240.refs_0_, ...), custom_call_target="tpu_custom_call", output_to_operand_aliasing={{0}: (7, {})} | custom-call | flops 8589934592 | bytes 20971520 | tf_op jit(solution)/shard_map/pallas_call | solution.py:171
  229.7 6.1 %collective-permute-done.35 = bf16[2048,256]{1,0:T(8,128)(2,1)} collective-permute-done((bf16[2048,256]{1,0:T(8,128)(2,1)}, bf16[2048,256]{1,0:T(8,128)(2,1)}, u32[]{:S(2)}, u32[]{:S(2)}) %collective-permute-start.35) | collective-permute-done | bytes 1048608 | tf_op jit(solution)/shard_map/ppermute | solution.py:233
  236.9 3.9 %broadcast_select_fusion = (bf16[2048,256]{1,0:T(8,128)(2,1)}, bf16[2048,256]{1,0:T(8,128)(2,1)S(1)}, bf16[2048,256]{1,0:T(8,128)(2,1)S(1)}, bf16[2048,256]{1,0:T(8,128)(2,1)}) fusion(pred[]{:T(512)S(6)} %eq.64, bf16[2048,256]{1,0:T(8,128)(2,1)} %collective-permute-done.32, bf16[2048,256]{1,0:T(8,128)(2,1)} %collective-permute-done.31, pred[]{:T(512)S(6)} %eq.59, ...), kind=kLoop, calls=%fused_computation.12 | loop fusion | flops 4194304 | bytes 10485762 | tf_op jit(solution)/shard_map/jit(_where)/select_n | solution.py:344
  242.0 3.4 %copy-done.4 = bf16[2048,2048]{1,0:T(8,128)(2,1)S(1)} copy-done((bf16[2048,2048]{1,0:T(8,128)(2,1)S(1)}, bf16[2048,2048]{1,0:T(8,128)(2,1)}, u32[]{:S(2)}) %copy-start.4) | copy-done | bytes 8388632
  245.4 7.2 %shard_map.35 = (f32[2048,4096]{1,0:T(8,128)}, f32[8,128]{1,0:T(8,128)}) custom-call(s32[2]{0:T(128)S(1)} %pad_add_fusion.4.blocks_ref, s32[1]{0:T(128)} %bitcast.2.place_ref, bf16[2048,2048]{1,0:T(8,128)(2,1)S(1)} %copy-done.4, bf16[2048,256]{1,0:T(8,128)(2,1)S(1)} %get-tuple-element.291.refs_0_, ...), custom_call_target="tpu_custom_call", output_to_operand_aliasing={{0}: (5, {})} | custom-call | flops 4294967296 | bytes 14680064 | tf_op jit(solution)/shard_map/pallas_call | solution.py:171
  252.6 8.4 %shard_map.36 = (f32[2048,4096]{1,0:T(8,128)}, f32[8,128]{1,0:T(8,128)}) custom-call(s32[2]{0:T(128)S(1)} %pad_add_fusion.blocks_ref, s32[1]{0:T(128)} %bitcast.2.place_ref, bf16[2048,2048]{1,0:T(8,128)(2,1)S(1)} %copy-done.4, bf16[2048,256]{1,0:T(8,128)(2,1)S(1)} %collective-permute-done.37.refs_0_, ...), custom_call_target="tpu_custom_call", output_to_operand_aliasing={{0}: (5, {})} | custom-call | flops 4294967296 | bytes 14680064 | tf_op jit(solution)/shard_map/pallas_call | solution.py:171
  (131 shorter events, 97.7 us)
Async XLA Ops:
  2.7 20.0 %collective-permute-start = (bf16[2048,256]{1,0:T(8,128)(2,1)S(1)}, bf16[2048,256]{1,0:T(8,128)(2,1)S(1)}, u32[]{:S(2)}, u32[]{:S(2)}) collective-permute-start(bf16[2048,256]{1,0:T(8,128)(2,1)S(1)} %get-tuple-element.159.refs_0_), channel_id=1, source_target_pairs={{1,3},{3,1},{5,7},{7,5},{9,11},{11,9},{13,15},{15,13},{17,19},{19,... | collective-permute-start | bytes 3145736 | tf_op jit(solution)/shard_map/ppermute | solution.py:233
  25.0 15.6 %collective-permute-start.2 = (bf16[2048,256]{1,0:T(8,128)(2,1)S(1)}, bf16[2048,256]{1,0:T(8,128)(2,1)}, u32[]{:S(2)}, u32[]{:S(2)}) collective-permute-start(bf16[2048,256]{1,0:T(8,128)(2,1)S(1)} %get-tuple-element.159.refs_0_), channel_id=1, source_target_pairs={{8,16},{9,17},{10,18},{11,19},{12,20},{13,21},{14,22},{15,23},{16,... | collective-permute-start | bytes 3145736 | tf_op jit(solution)/shard_map/ppermute | solution.py:233
  42.4 18.2 %collective-permute-start.6 = (bf16[2048,256]{1,0:T(8,128)(2,1)}, bf16[2048,256]{1,0:T(8,128)(2,1)}, u32[]{:S(2)}, u32[]{:S(2)}) collective-permute-start(bf16[2048,256]{1,0:T(8,128)(2,1)} %collective-permute-done.2), channel_id=1, source_target_pairs={{8,0},{9,1},{10,2},{11,3},{12,4},{13,5},{14,6},{15,7},{16,24},{17,... | collective-permute-start | bytes 3145736 | tf_op jit(solution)/shard_map/ppermute | solution.py:233
  48.7 17.5 %collective-permute-start.7 = (bf16[2048,256]{1,0:T(8,128)(2,1)}, bf16[2048,256]{1,0:T(8,128)(2,1)}, u32[]{:S(2)}, u32[]{:S(2)}) collective-permute-start(bf16[2048,256]{1,0:T(8,128)(2,1)} %collective-permute-done.1), channel_id=1, source_target_pairs={{8,16},{9,17},{10,18},{11,19},{12,20},{13,21},{14,22},{15,23},{16,... | collective-permute-start | bytes 3145736 | tf_op jit(solution)/shard_map/ppermute | solution.py:233
  69.3 18.3 %collective-permute-start.12 = (bf16[2048,256]{1,0:T(8,128)(2,1)S(1)}, bf16[2048,256]{1,0:T(8,128)(2,1)}, u32[]{:S(2)}, u32[]{:S(2)}) collective-permute-start(bf16[2048,256]{1,0:T(8,128)(2,1)S(1)} %get-tuple-element.218.refs_1_), channel_id=1, source_target_pairs={{8,16},{9,17},{10,18},{11,19},{12,20},{13,21},{14,22},{15,23},{16,... | collective-permute-start | bytes 3145736 | tf_op jit(solution)/shard_map/ppermute | solution.py:233
  75.8 16.6 %collective-permute-start.13 = (bf16[2048,256]{1,0:T(8,128)(2,1)}, bf16[2048,256]{1,0:T(8,128)(2,1)}, u32[]{:S(2)}, u32[]{:S(2)}) collective-permute-start(bf16[2048,256]{1,0:T(8,128)(2,1)} %get-tuple-element.276), channel_id=1, source_target_pairs={{0,4},{1,5},{2,6},{3,7},{4,0},{5,1},{6,2},{7,3},{8,12},{9,13},{10,... | collective-permute-start | bytes 3145736 | tf_op jit(solution)/shard_map/ppermute | solution.py:233
  76.5 15.9 %collective-permute-start.14 = (bf16[2048,256]{1,0:T(8,128)(2,1)}, bf16[2048,256]{1,0:T(8,128)(2,1)}, u32[]{:S(2)}, u32[]{:S(2)}) collective-permute-start(bf16[2048,256]{1,0:T(8,128)(2,1)} %get-tuple-element.275), channel_id=1, source_target_pairs={{0,2},{1,3},{2,0},{3,1},{4,6},{5,7},{6,4},{7,5},{8,10},{9,11},{10,... | collective-permute-start | bytes 3145736 | tf_op jit(solution)/shard_map/ppermute | solution.py:233
  97.2 17.0 %collective-permute-start.16 = (bf16[2048,256]{1,0:T(8,128)(2,1)S(1)}, bf16[2048,256]{1,0:T(8,128)(2,1)S(1)}, u32[]{:S(2)}, u32[]{:S(2)}) collective-permute-start(bf16[2048,256]{1,0:T(8,128)(2,1)S(1)} %get-tuple-element.298), channel_id=1, source_target_pairs={{0,4},{1,5},{2,6},{3,7},{4,0},{5,1},{6,2},{7,3},{8,12},{9,13},{10,... | collective-permute-start | bytes 3145736 | tf_op jit(solution)/shard_map/ppermute | solution.py:233
  98.9 17.2 %collective-permute-start.17 = (bf16[2048,256]{1,0:T(8,128)(2,1)S(1)}, bf16[2048,256]{1,0:T(8,128)(2,1)S(1)}, u32[]{:S(2)}, u32[]{:S(2)}) collective-permute-start(bf16[2048,256]{1,0:T(8,128)(2,1)S(1)} %get-tuple-element.289), channel_id=1, source_target_pairs={{0,2},{1,3},{2,0},{3,1},{4,6},{5,7},{6,4},{7,5},{8,10},{9,11},{10,... | collective-permute-start | bytes 3145736 | tf_op jit(solution)/shard_map/ppermute | solution.py:233
  99.7 16.9 %collective-permute-start.18 = (bf16[2048,256]{1,0:T(8,128)(2,1)S(1)}, bf16[2048,256]{1,0:T(8,128)(2,1)S(1)}, u32[]{:S(2)}, u32[]{:S(2)}) collective-permute-start(bf16[2048,256]{1,0:T(8,128)(2,1)S(1)} %get-tuple-element.218.refs_1_), channel_id=1, source_target_pairs={{0,8},{1,9},{2,10},{3,11},{4,12},{5,13},{6,14},{7,15},{8,0},{9,1},... | collective-permute-start | bytes 3145736 | tf_op jit(solution)/shard_map/ppermute | solution.py:233
  99.7 16.9 %collective-permute-start.19 = (bf16[2048,256]{1,0:T(8,128)(2,1)S(1)}, bf16[2048,256]{1,0:T(8,128)(2,1)S(1)}, u32[]{:S(2)}, u32[]{:S(2)}) collective-permute-start(bf16[2048,256]{1,0:T(8,128)(2,1)S(1)} %copy-done.6), channel_id=1, source_target_pairs={{0,1},{1,0},{2,3},{3,2},{4,5},{5,4},{6,7},{7,6},{8,9},{9,8},{10,11... | collective-permute-start | bytes 3145736 | tf_op jit(solution)/shard_map/ppermute | solution.py:233
  99.7 16.9 %collective-permute-start.20 = (bf16[2048,256]{1,0:T(8,128)(2,1)S(1)}, bf16[2048,256]{1,0:T(8,128)(2,1)S(1)}, u32[]{:S(2)}, u32[]{:S(2)}) collective-permute-start(bf16[2048,256]{1,0:T(8,128)(2,1)S(1)} %get-tuple-element.266), channel_id=1, source_target_pairs={{0,1},{1,0},{2,3},{3,2},{4,5},{5,4},{6,7},{7,6},{8,9},{9,8},{10,11... | collective-permute-start | bytes 3145736 | tf_op jit(solution)/shard_map/ppermute | solution.py:233
  116.6 19.9 %collective-permute-start.21 = (bf16[2048,256]{1,0:T(8,128)(2,1)}, bf16[2048,256]{1,0:T(8,128)(2,1)S(1)}, u32[]{:S(2)}, u32[]{:S(2)}) collective-permute-start(bf16[2048,256]{1,0:T(8,128)(2,1)} %collective-permute-done.12), channel_id=1, source_target_pairs={{8,0},{9,1},{10,2},{11,3},{12,4},{13,5},{14,6},{15,7},{16,24},{17,... | collective-permute-start | bytes 3145736 | tf_op jit(solution)/shard_map/ppermute | solution.py:233
  120.8 16.3 %collective-permute-start.22 = (bf16[2048,256]{1,0:T(8,128)(2,1)S(1)}, bf16[2048,256]{1,0:T(8,128)(2,1)}, u32[]{:S(2)}, u32[]{:S(2)}) collective-permute-start(bf16[2048,256]{1,0:T(8,128)(2,1)S(1)} %collective-permute-done.18), channel_id=1, source_target_pairs={{8,16},{9,17},{10,18},{11,19},{12,20},{13,21},{14,22},{15,23},{16,... | collective-permute-start | bytes 3145736 | tf_op jit(solution)/shard_map/ppermute | solution.py:233
  140.9 34.1 %collective-permute-start.26 = (bf16[2048,256]{1,0:T(8,128)(2,1)}, bf16[2048,256]{1,0:T(8,128)(2,1)}, u32[]{:S(2)}, u32[]{:S(2)}) collective-permute-start(bf16[2048,256]{1,0:T(8,128)(2,1)} %collective-permute-done.22), channel_id=1, source_target_pairs={{8,0},{9,1},{10,2},{11,3},{12,4},{13,5},{14,6},{15,7},{16,24},{17,... | collective-permute-start | bytes 3145736 | tf_op jit(solution)/shard_map/ppermute | solution.py:233
  146.0 29.0 %collective-permute-start.27 = (bf16[2048,256]{1,0:T(8,128)(2,1)}, bf16[2048,256]{1,0:T(8,128)(2,1)}, u32[]{:S(2)}, u32[]{:S(2)}) collective-permute-start(bf16[2048,256]{1,0:T(8,128)(2,1)} %get-tuple-element.274), channel_id=1, source_target_pairs={{0,4},{1,5},{2,6},{3,7},{4,0},{5,1},{6,2},{7,3},{8,12},{9,13},{10,... | collective-permute-start | bytes 3145736 | tf_op jit(solution)/shard_map/ppermute | solution.py:233
  148.9 26.1 %collective-permute-start.28 = (bf16[2048,256]{1,0:T(8,128)(2,1)}, bf16[2048,256]{1,0:T(8,128)(2,1)}, u32[]{:S(2)}, u32[]{:S(2)}) collective-permute-start(bf16[2048,256]{1,0:T(8,128)(2,1)} %get-tuple-element.273), channel_id=1, source_target_pairs={{0,2},{1,3},{2,0},{3,1},{4,6},{5,7},{6,4},{7,5},{8,10},{9,11},{10,... | collective-permute-start | bytes 3145736 | tf_op jit(solution)/shard_map/ppermute | solution.py:233
  154.1 20.9 %collective-permute-start.29 = (bf16[2048,256]{1,0:T(8,128)(2,1)}, bf16[2048,256]{1,0:T(8,128)(2,1)}, u32[]{:S(2)}, u32[]{:S(2)}) collective-permute-start(bf16[2048,256]{1,0:T(8,128)(2,1)} %get-tuple-element.296), channel_id=1, source_target_pairs={{0,1},{1,0},{2,3},{3,2},{4,5},{5,4},{6,7},{7,6},{8,9},{9,8},{10,11... | collective-permute-start | bytes 3145736 | tf_op jit(solution)/shard_map/ppermute | solution.py:233
  154.2 20.8 %collective-permute-start.30 = (bf16[2048,256]{1,0:T(8,128)(2,1)}, bf16[2048,256]{1,0:T(8,128)(2,1)}, u32[]{:S(2)}, u32[]{:S(2)}) collective-permute-start(bf16[2048,256]{1,0:T(8,128)(2,1)} %get-tuple-element.271), channel_id=1, source_target_pairs={{0,1},{1,0},{2,3},{3,2},{4,5},{5,4},{6,7},{7,6},{8,9},{9,8},{10,11... | collective-permute-start | bytes 3145736 | tf_op jit(solution)/shard_map/ppermute | solution.py:233
  181.2 25.1 %collective-permute-start.31 = (bf16[2048,256]{1,0:T(8,128)(2,1)}, bf16[2048,256]{1,0:T(8,128)(2,1)}, u32[]{:S(2)}, u32[]{:S(2)}) collective-permute-start(bf16[2048,256]{1,0:T(8,128)(2,1)} %get-tuple-element.294), channel_id=1, source_target_pairs={{0,4},{1,5},{2,6},{3,7},{4,0},{5,1},{6,2},{7,3},{8,12},{9,13},{10,... | collective-permute-start | bytes 3145736 | tf_op jit(solution)/shard_map/ppermute | solution.py:233
  181.2 25.0 %collective-permute-start.32 = (bf16[2048,256]{1,0:T(8,128)(2,1)}, bf16[2048,256]{1,0:T(8,128)(2,1)}, u32[]{:S(2)}, u32[]{:S(2)}) collective-permute-start(bf16[2048,256]{1,0:T(8,128)(2,1)} %get-tuple-element.287), channel_id=1, source_target_pairs={{0,2},{1,3},{2,0},{3,1},{4,6},{5,7},{6,4},{7,5},{8,10},{9,11},{10,... | collective-permute-start | bytes 3145736 | tf_op jit(solution)/shard_map/ppermute | solution.py:233
  181.2 25.0 %collective-permute-start.33 = (bf16[2048,256]{1,0:T(8,128)(2,1)}, bf16[2048,256]{1,0:T(8,128)(2,1)}, u32[]{:S(2)}, u32[]{:S(2)}) collective-permute-start(bf16[2048,256]{1,0:T(8,128)(2,1)} %get-tuple-element.263), channel_id=1, source_target_pairs={{0,1},{1,0},{2,3},{3,2},{4,5},{5,4},{6,7},{7,6},{8,9},{9,8},{10,11... | collective-permute-start | bytes 3145736 | tf_op jit(solution)/shard_map/ppermute | solution.py:233
  210.6 25.1 %collective-permute-start.35 = (bf16[2048,256]{1,0:T(8,128)(2,1)}, bf16[2048,256]{1,0:T(8,128)(2,1)}, u32[]{:S(2)}, u32[]{:S(2)}) collective-permute-start(bf16[2048,256]{1,0:T(8,128)(2,1)} %get-tuple-element.293), channel_id=1, source_target_pairs={{0,4},{1,5},{2,6},{3,7},{4,0},{5,1},{6,2},{7,3},{8,12},{9,13},{10,... | collective-permute-start | bytes 3145736 | tf_op jit(solution)/shard_map/ppermute | solution.py:233
  212.1 24.8 %collective-permute-start.36 = (bf16[2048,256]{1,0:T(8,128)(2,1)}, bf16[2048,256]{1,0:T(8,128)(2,1)}, u32[]{:S(2)}, u32[]{:S(2)}) collective-permute-start(bf16[2048,256]{1,0:T(8,128)(2,1)} %collective-permute-done.31), channel_id=1, source_target_pairs={{0,2},{1,3},{2,0},{3,1},{4,6},{5,7},{6,4},{7,5},{8,10},{9,11},{10,... | collective-permute-start | bytes 3145736 | tf_op jit(solution)/shard_map/ppermute | solution.py:233
  (40 other events, 435.3 us)
